TPU v7x, 32 devices: a whole 2x2x4 slice. The times are simulated.
32 devices in a mesh: dp: 8 (over z, x), ctx: 4 (over y, core).
Axes of the slice: x: 2, y: 2, z: 4, core: 2. Of those that a mesh axis runs over, the one named last changes fastest.
Arguments:
- tokens: bfloat16 [16, 1024, 1088], P('dp', 'ctx'), may hold values from -6 to 6
- positions: int32 [16, 1024], P('dp'), may hold values from 0 to 1023, as said below
- w_qkv: bfloat16 [3551232], P(('dp', 'ctx')), may hold values from -0.1875 to 0.1875
- w_out: bfloat16 [1183744], P(('dp', 'ctx')), may hold values from -0.75 to 0.75
- w_up: bfloat16 [4734976], P(('dp', 'ctx')), may hold values from -0.1875 to 0.1875
- w_down: bfloat16 [4734976], P(('dp', 'ctx')), may hold values from -0.09375 to 0.09375
- small_params: bfloat16 [13056], P(('dp', 'ctx')), may hold values from -1.2 to 1.6, as said below
- cotangent: bfloat16 [16, 1024, 1088], P('dp', 'ctx'), may hold values from -6 to 6
Outputs:
- result: bfloat16 [16, 1024, 1088], P('dp', 'ctx')
- grad_tokens: bfloat16 [16, 1024, 1088], P('dp', 'ctx')
- grad_qkv: float32 [3551232], P(('dp', 'ctx'))
- grad_out: float32 [1183744], P(('dp', 'ctx'))
- grad_up: float32 [4734976], P(('dp', 'ctx'))
- grad_down: float32 [4734976], P(('dp', 'ctx'))
- grad_small: float32 [13056], P(('dp', 'ctx'))
Inputs may be any that keep to these rules, and one draw needn't show every extreme that they name: Each row is a permutation of 0 to 1023. Spans are runs of 128 positions; slot block c (slots c * 2 * 128 onward) holds, in rising order, span j and then span 2 * 4 - 1 - j, with j differing between blocks and sequences. `small_params`: gains near one and biases of either sign, in the layout of the argument.
All inputs are finite; a program needn't handle non-finite values.
Results may differ from a plain program's by a relative error of at most 0.013.
Values may be sent and summed in bfloat16 or wider, within the bound.
No kernel may reach another device: no remote copies, remote signals or barrier semaphores. Data moves between devices by JAX's collectives and lax.ppermute only.
A program may use at most 256 MiB of HBM per device.

v0:
```python
import jax
import jax.numpy as jnp
from jax import lax
from jax.sharding import PartitionSpec as P

HEADS = 17
HEAD_DIM = 64
FF = 4352
MICRO = 2


def layer_stats(values):
    center = values - jnp.mean(values, axis=-1, keepdims=True)
    inverse = lax.rsqrt(jnp.mean(center * center, axis=-1, keepdims=True) + 1e-05)
    return (center * inverse, inverse)


def norm_back(upstream, normed, inverse, gain_vector):
    scaled = upstream * gain_vector
    return inverse * (
        scaled
        - jnp.mean(scaled, axis=-1, keepdims=True)
        - normed * jnp.mean(scaled * normed, axis=-1, keepdims=True)
    )


def lead_dot(left_side, right_side):
    return lax.dot_general(
        left_side, right_side, (((0,), (0,)), ((), ())), preferred_element_type=jnp.float32
    )


def tail_dot(left_side, right_side):
    return lax.dot_general(
        left_side, right_side, (((1,), (1,)), ((), ())), preferred_element_type=jnp.float32
    )


def smooth_gate(values):
    return jax.nn.gelu(values, approximate=True)


def as_rows(values):
    return values.reshape(1, -1)


def unpack(gathered, model_width, hidden_width):
    qkv_mat, out_mat, up_mat, down_mat, packed = gathered
    packed = packed.reshape(-1).astype(jnp.float32)
    pieces = [packed[number * model_width : (number + 1) * model_width] for number in range(7)]
    up_bias = packed[7 * model_width : 7 * model_width + hidden_width]
    down_bias = packed[7 * model_width + hidden_width :]
    return (
        qkv_mat.reshape(model_width, 3 * model_width),
        out_mat.reshape(model_width, model_width),
        up_mat.reshape(model_width, hidden_width),
        down_mat.reshape(hidden_width, model_width),
        pieces,
        up_bias,
        down_bias,
    )


def masked_scores(query, keys_all, allowed, factor):
    scores = (
        jnp.einsum("bqhd,bkhd->bhqk", query, keys_all, preferred_element_type=jnp.float32) * factor
    )
    return jnp.where(allowed, scores, -1e30)


def local(tokens, positions, w_qkv, w_out, w_up, w_down, small_params, cotangent):
    seqs_here, local_len, model_width = tokens.shape
    group_size = seqs_here // MICRO
    block_rows = group_size * local_len
    factor = HEAD_DIM ** (-0.5)
    owners = lax.axis_size(("dp", "ctx"))
    start_here = lax.axis_index("ctx") * local_len
    shard_rows = (
        as_rows(w_qkv),
        as_rows(w_out),
        as_rows(w_up),
        as_rows(w_down),
        as_rows(small_params),
    )
    acc_qkv = jnp.zeros((model_width, 3 * model_width), jnp.float32)
    acc_out = jnp.zeros((model_width, model_width), jnp.float32)
    acc_up = jnp.zeros((model_width, FF), jnp.float32)
    acc_down = jnp.zeros((FF, model_width), jnp.float32)
    acc_small = [jnp.zeros((model_width,), jnp.float32) for number in range(7)]
    acc_upbias = jnp.zeros((FF,), jnp.float32)
    acc_downbias = jnp.zeros((model_width,), jnp.float32)
    result_parts = []
    grad_parts = []
    for micro_step in range(MICRO):
        params_now = unpack(
            (
                lax.all_gather(shard_rows[0], ("dp", "ctx"), axis=0, tiled=True),
                lax.all_gather(shard_rows[1], ("dp", "ctx"), axis=0, tiled=True),
                lax.all_gather(shard_rows[2], ("dp", "ctx"), axis=0, tiled=True),
                lax.all_gather(shard_rows[3], ("dp", "ctx"), axis=0, tiled=True),
                lax.all_gather(shard_rows[4], ("dp", "ctx"), axis=0, tiled=True),
            ),
            model_width,
            FF,
        )
        qkv_mat, out_mat, up_mat, down_mat, pieces, up_bias, down_bias = params_now
        gain_one, bias_one, bias_query, bias_value, bias_out, gain_two, bias_two = pieces
        lower_seq = micro_step * group_size
        upper_seq = lower_seq + group_size
        inputs_now = (
            tokens[lower_seq:upper_seq].reshape(block_rows, model_width).astype(jnp.float32)
        )
        place_rows = positions[lower_seq:upper_seq]
        query_places = lax.dynamic_slice_in_dim(place_rows, start_here, local_len, 1)
        allowed = place_rows[:, None, None, :] <= query_places[:, None, :, None]
        normed_one, inverse_one = layer_stats(inputs_now)
        act_one = (normed_one * gain_one + bias_one).astype(jnp.bfloat16)
        qkv_bias = jnp.concatenate([bias_query, jnp.zeros_like(bias_query), bias_value])
        qkv_rows = (
            jnp.dot(act_one, qkv_mat, preferred_element_type=jnp.float32) + qkv_bias
        ).astype(jnp.bfloat16)
        qkv_rows = qkv_rows.reshape(group_size, local_len, 3, HEADS, HEAD_DIM)
        query = qkv_rows[:, :, 0]
        key_local = qkv_rows[:, :, 1]
        value_local = qkv_rows[:, :, 2]
        keys_all, values_all = (
            lax.all_gather(key_local, "ctx", axis=1, tiled=True),
            lax.all_gather(value_local, "ctx", axis=1, tiled=True),
        )
        scores = masked_scores(query, keys_all, allowed, factor)
        top_score = jnp.max(scores, axis=-1, keepdims=True)
        expo = jnp.exp(scores - top_score)
        denom = jnp.sum(expo, axis=-1, keepdims=True)
        probs = expo / denom
        log_total = top_score + jnp.log(denom)
        mixed = jnp.einsum(
            "bhqk,bkhd->bqhd",
            probs.astype(jnp.bfloat16),
            values_all,
            preferred_element_type=jnp.float32,
        )
        mixed = mixed.astype(jnp.bfloat16).reshape(block_rows, model_width)
        resid = inputs_now + jnp.dot(mixed, out_mat, preferred_element_type=jnp.float32) + bias_out
        normed_two, inverse_two = layer_stats(resid)
        act_two = (normed_two * gain_two + bias_two).astype(jnp.bfloat16)
        pre_act = jnp.dot(act_two, up_mat, preferred_element_type=jnp.float32) + up_bias
        gelu_rows = smooth_gate(pre_act).astype(jnp.bfloat16)
        outputs_now = (
            resid + jnp.dot(gelu_rows, down_mat, preferred_element_type=jnp.float32) + down_bias
        )
        result_parts.append(outputs_now.astype(jnp.bfloat16))
        qkv_mat, out_mat, up_mat, down_mat, pieces, up_bias, down_bias = unpack(
            (
                lax.all_gather(shard_rows[0], ("dp", "ctx"), axis=0, tiled=True),
                lax.all_gather(shard_rows[1], ("dp", "ctx"), axis=0, tiled=True),
                lax.all_gather(shard_rows[2], ("dp", "ctx"), axis=0, tiled=True),
                lax.all_gather(shard_rows[3], ("dp", "ctx"), axis=0, tiled=True),
                lax.all_gather(shard_rows[4], ("dp", "ctx"), axis=0, tiled=True),
            ),
            model_width,
            FF,
        )
        gain_one = pieces[0]
        gain_two = pieces[5]
        grad_rows = cotangent[lower_seq:upper_seq].reshape(block_rows, model_width)
        grad_float = grad_rows.astype(jnp.float32)
        acc_down = acc_down + lead_dot(gelu_rows, grad_rows)
        acc_downbias = acc_downbias + jnp.sum(grad_float, axis=0)
        grad_gelu = tail_dot(grad_rows, down_mat)
        gelu_pull = jax.vjp(smooth_gate, pre_act)[1]
        grad_pre = gelu_pull(grad_gelu)[0].astype(jnp.bfloat16)
        acc_up = acc_up + lead_dot(act_two, grad_pre)
        acc_upbias = acc_upbias + jnp.sum(grad_pre.astype(jnp.float32), axis=0)
        grad_act_two = tail_dot(grad_pre, up_mat)
        gain_two_term = jnp.sum(grad_act_two * normed_two, axis=0)
        bias_two_term = jnp.sum(grad_act_two, axis=0)
        grad_resid = grad_float + norm_back(grad_act_two, normed_two, inverse_two, gain_two)
        grad_attn = grad_resid.astype(jnp.bfloat16)
        acc_out = acc_out + lead_dot(mixed, grad_attn)
        bias_out_term = jnp.sum(grad_attn.astype(jnp.float32), axis=0)
        grad_mixed = (
            tail_dot(grad_attn, out_mat)
            .astype(jnp.bfloat16)
            .reshape(group_size, local_len, HEADS, HEAD_DIM)
        )
        probs_again = jnp.exp(masked_scores(query, keys_all, allowed, factor) - log_total)
        grad_probs = jnp.einsum(
            "bqhd,bkhd->bhqk", grad_mixed, values_all, preferred_element_type=jnp.float32
        )
        grad_scores = probs_again * (
            grad_probs - jnp.sum(grad_probs * probs_again, axis=-1, keepdims=True)
        )
        grad_scores = grad_scores.astype(jnp.bfloat16)
        grad_query = (
            jnp.einsum("bhqk,bkhd->bqhd", grad_scores, keys_all, preferred_element_type=jnp.float32)
            * factor
        )
        key_terms = (
            jnp.einsum("bhqk,bqhd->bkhd", grad_scores, query, preferred_element_type=jnp.float32)
            * factor
        )
        value_terms = jnp.einsum(
            "bhqk,bqhd->bkhd",
            probs_again.astype(jnp.bfloat16),
            grad_mixed,
            preferred_element_type=jnp.float32,
        )
        grad_key, grad_value = (
            lax.psum_scatter(
                key_terms.astype(jnp.bfloat16), "ctx", scatter_dimension=1, tiled=True
            ).astype(jnp.float32),
            lax.psum_scatter(
                value_terms.astype(jnp.bfloat16), "ctx", scatter_dimension=1, tiled=True
            ).astype(jnp.float32),
        )
        grad_qkv_rows = jnp.stack([grad_query, grad_key, grad_value], axis=2).astype(jnp.bfloat16)
        grad_qkv_rows = grad_qkv_rows.reshape(block_rows, 3 * model_width)
        acc_qkv = acc_qkv + lead_dot(act_one, grad_qkv_rows)
        qkv_sums = jnp.sum(grad_qkv_rows.astype(jnp.float32), axis=0)
        grad_act_one = tail_dot(grad_qkv_rows, qkv_mat)
        gain_one_term = jnp.sum(grad_act_one * normed_one, axis=0)
        bias_one_term = jnp.sum(grad_act_one, axis=0)
        grad_input = grad_resid + norm_back(grad_act_one, normed_one, inverse_one, gain_one)
        grad_parts.append(grad_input.astype(jnp.bfloat16))
        new_terms = [
            gain_one_term,
            bias_one_term,
            qkv_sums[:model_width],
            qkv_sums[2 * model_width :],
            bias_out_term,
            gain_two_term,
            bias_two_term,
        ]
        acc_small = [older + newer for older, newer in zip(acc_small, new_terms)]
    result = jnp.concatenate(result_parts, axis=0).reshape(seqs_here, local_len, model_width)
    grad_tokens = jnp.concatenate(grad_parts, axis=0).reshape(seqs_here, local_len, model_width)
    small_grad = jnp.concatenate(acc_small + [acc_upbias, acc_downbias])
    summed = (
        lax.psum_scatter(
            acc_qkv.reshape(owners, -1), ("dp", "ctx"), scatter_dimension=0, tiled=True
        ),
        lax.psum_scatter(
            acc_out.reshape(owners, -1), ("dp", "ctx"), scatter_dimension=0, tiled=True
        ),
        lax.psum_scatter(
            acc_up.reshape(owners, -1), ("dp", "ctx"), scatter_dimension=0, tiled=True
        ),
        lax.psum_scatter(
            acc_down.reshape(owners, -1), ("dp", "ctx"), scatter_dimension=0, tiled=True
        ),
        lax.psum_scatter(
            small_grad.reshape(owners, -1), ("dp", "ctx"), scatter_dimension=0, tiled=True
        ),
    )
    grad_qkv, grad_out, grad_up, grad_down, grad_small = [piece.reshape(-1) for piece in summed]
    return (result, grad_tokens, grad_qkv, grad_out, grad_up, grad_down, grad_small)


def solution(mesh):
    return jax.shard_map(
        local,
        mesh=mesh,
        in_specs=(
            P("dp", "ctx", None),
            P("dp", None),
            P(("dp", "ctx")),
            P(("dp", "ctx")),
            P(("dp", "ctx")),
            P(("dp", "ctx")),
            P(("dp", "ctx")),
            P("dp", "ctx", None),
        ),
        out_specs=(
            P("dp", "ctx", None),
            P("dp", "ctx", None),
            P(("dp", "ctx")),
            P(("dp", "ctx")),
            P(("dp", "ctx")),
            P(("dp", "ctx")),
            P(("dp", "ctx")),
        ),
        check_vma=False,
    )
```

profile of v0, /device:TPU:0, one launch (start us, length us, event | category | flops | bytes accessed | tf_op | source)
XLA Modules:
  0.0 1998.4 jit_solution(1975548961361951668)
XLA Ops:
  11.9 42.8 %all-reduce = bf16[13056]{0:T(1024)(128)(2,1)S(1)} all-reduce(bf16[13056]{0:T(1024)(128)(2,1)S(1)} %dynamic-update-slice), channel_id=2, replica_groups=mesh['dp'=8,'ctx'=4] {'dp','ctx'}, use_global_device_ids=true, to_apply=%add | all-reduce | flops 13056 | bytes 52224
  56.1 62.4 %all-gather.30.cloned.1.call-done = bf16[32,1,110976]{2,1,0:T(2,128)(2,1)} async-done(((bf16[1,1,110976]{2,1,0:T(2,128)(2,1)}), bf16[32,1,110976]{2,1,0:T(2,128)(2,1)}) %all-gather.30.cloned.1.call-update) | async-done | bytes 7102480 | tf_op jit(solution)/shard_map/all_gather | solution.py:97
  118.5 129.7 %reduce.16 = bf16[32,110976]{1,0:T(8,128)(2,1)} reduce(bf16[32,1,110976]{2,1,0:T(2,128)(2,1)} %all-gather.30.cloned.1.call-done, bf16[]{:T(256)} %constant.77), dimensions={1}, to_apply=%all-gather.9.reduce_sub_computation | reduce | bytes 14204930 | tf_op jit(solution)/shard_map/all_gather | solution.py:97
  288.9 49.4 %reduce.17 = bf16[32,36992]{1,0:T(8,128)(2,1)S(1)} reduce(bf16[32,1,36992]{2,1,0:T(2,128)(2,1)} %all-gather.32.cloned.1.call-done, bf16[]{:T(256)} %constant.77), dimensions={1}, to_apply=%all-gather.10.reduce_sub_computation | reduce | bytes 4734978 | tf_op jit(solution)/shard_map/all_gather | solution.py:98
  341.9 11.4 fusion.144
  405.0 88.8 %all-gather.34.cloned.1.call-done = bf16[32,1,147968]{2,1,0:T(2,128)(2,1)} async-done(((bf16[1,1,147968]{2,1,0:T(2,128)(2,1)}), bf16[32,1,147968]{2,1,0:T(2,128)(2,1)}) %all-gather.34.cloned.1.call-update) | async-done | bytes 9469968 | tf_op jit(solution)/shard_map/all_gather | solution.py:99
  493.8 156.0 %reduce.18 = bf16[32,147968]{1,0:T(8,128)(2,1)} reduce(bf16[32,1,147968]{2,1,0:T(2,128)(2,1)} %all-gather.34.cloned.1.call-done, bf16[]{:T(256)} %constant.77), dimensions={1}, to_apply=%all-gather.11.reduce_sub_computation | reduce | bytes 18939906 | tf_op jit(solution)/shard_map/all_gather | solution.py:99
  649.8 17.6 reshape.750
  667.5 156.1 %reduce.19 = bf16[32,147968]{1,0:T(8,128)(2,1)} reduce(bf16[32,1,147968]{2,1,0:T(2,128)(2,1)} %all-gather.36.cloned.1.call-done, bf16[]{:T(256)} %constant.77), dimensions={1}, to_apply=%all-gather.12.reduce_sub_computation | reduce | bytes 18939906 | tf_op jit(solution)/shard_map/all_gather | solution.py:100
  823.6 11.9 reshape.752
  888.8 13.7 multiply_reduce_fusion.1
  902.5 12.9 multiply_convert_fusion.1
  923.0 11.8 fusion.117
  934.9 12.6 convolution_add_fusion
  947.5 21.4 %copy.20 = f32[4352,1088]{1,0:T(8,128)} copy(f32[4352,1088]{0,1:T(8,128)} %convolution_add_fusion) | data formatting | bytes 37879808 | tf_op jit(solution)/shard_map/add | solution.py:167
  968.9 24.6 %reshape.770 = f32[32,147968]{1,0:T(8,128)} reshape(f32[4352,1088]{1,0:T(8,128)} %copy.20) | data formatting | bytes 37879808 | tf_op jit(solution)/shard_map/reshape | solution.py:249
  1009.0 13.9 multiply_reduce_fusion
  1035.0 12.6 multiply_convert_fusion
  1063.8 14.8 convolution_add_fusion.1
  1078.6 24.5 %reshape.768 = f32[32,147968]{1,0:T(8,128)} reshape(f32[1088,4352]{1,0:T(8,128)} %convolution_add_fusion.1) | data formatting | bytes 37879808 | tf_op jit(solution)/shard_map/reshape | solution.py:246
  1140.9 14.7 reshape.764
  1156.2 10.9 fusion.33
  1192.7 39.3 %all-reduce.5 = f32[32,408]{1,0:T(8,128)S(1)} all-reduce(f32[32,408]{1,0:T(8,128)S(1)} %reshape.772), channel_id=19, replica_groups=mesh['dp'=8,'ctx'=4] {'dp','ctx'}, use_global_device_ids=true, to_apply=%region_46.47.clone | all-reduce | flops 13056 | bytes 104448
  1232.7 735.3 %all-reduce.9.cloned.1.call-done = (f32[32,110976]{1,0:T(8,128)}, f32[32,36992]{1,0:T(8,128)}, f32[32,147968]{1,0:T(8,128)}, f32[32,147968]{1,0:T(8,128)}) async-done(((f32[32,110976]{1,0:T(8,128)}, f32[32,36992]{1,0:T(8,128)}, f32[32,147968]{1,0:T(8,128)}, f32[32,147968]{1,0:T(8,128)}), (f32[32,110976]{1,0:T(8,128)}, f32[32,36992]{1,0:T(8,128)}, f32[32,147968]{1,0:T(8,128)}, ...) | async-done | bytes 56819728
  (287 shorter events, 293.6 us)
Async XLA Ops:
  7.2 48.3 %copy-start.2 = (bf16[2,256,1088]{1,2,0:T(8,128)(2,1)S(1)}, bf16[2,256,1088]{1,2,0:T(8,128)(2,1)}, u32[]{:S(2)}) copy-start(bf16[2,256,1088]{1,2,0:T(8,128)(2,1)} %param.8) | copy-start | bytes 3342340
  7.2 111.3 %all-gather.30.cloned.1.call-start = ((), (), s32[]{:S(2)}) async-start(), calls=%async_computation.12 | async-start | bytes 14648832 | tf_op jit(solution)/shard_map/all_gather | solution.py:97
  9.3 279.6 %all-gather.32.cloned.1.call-start = ((), (), s32[]{:S(2)}) async-start(), calls=%async_computation.13 | async-start | bytes 4882944 | tf_op jit(solution)/shard_map/all_gather | solution.py:98
  11.0 330.9 %all-gather.24.cloned.1.call-start = ((), (), s32[]{:S(2)}) async-start(), calls=%async_computation.9 | async-start | bytes 2785280 | tf_op jit(solution)/shard_map/all_gather | solution.py:127
  55.4 212.4 %copy-start.42 = (f32[1088]{0:T(1024)}, f32[1088]{0:T(1024)S(1)}, u32[]{:S(2)}) copy-start(f32[1088]{0:T(1024)S(1)} %get-tuple-element.83) | copy-start | bytes 13060
  55.4 212.4 %copy-start.44 = (f32[1088]{0:T(1024)}, f32[1088]{0:T(1024)S(1)}, u32[]{:S(2)}) copy-start(f32[1088]{0:T(1024)S(1)} %get-tuple-element.82) | copy-start | bytes 13060
  55.4 786.1 %copy-start.36 = (f32[1088]{0:T(1024)}, f32[1088]{0:T(1024)S(1)}, u32[]{:S(2)}) copy-start(f32[1088]{0:T(1024)S(1)} %get-tuple-element.79) | copy-start | bytes 13060
  55.7 202.3 %copy-start.46 = (f32[256]{0:T(256)}, f32[256]{0:T(256)S(1)}, u32[]{:S(2)}) copy-start(f32[256]{0:T(256)S(1)} %get-tuple-element.111) | copy-start | bytes 3076
  55.7 212.1 %copy-start.52 = (f32[256]{0:T(256)}, f32[256]{0:T(256)S(1)}, u32[]{:S(2)}) copy-start(f32[256]{0:T(256)S(1)} %get-tuple-element.110) | copy-start | bytes 3076
  56.1 202.0 %copy-start.54 = (f32[256]{0:T(256)}, f32[256]{0:T(256)S(1)}, u32[]{:S(2)}) copy-start(f32[256]{0:T(256)S(1)} %add_rsqrt_fusion.3) | copy-start | bytes 3076
  267.1 95.2 %all-gather.22.cloned.1.call-start = ((), (), s32[]{:S(2)}) async-start(), calls=%async_computation.8 | async-start | bytes 2785280 | tf_op jit(solution)/shard_map/all_gather | solution.py:128
  267.7 106.2 %all-gather.28.cloned.1.call-start = ((), (), s32[]{:S(2)}) async-start(), calls=%async_computation.11 | async-start | bytes 2785280 | tf_op jit(solution)/shard_map/all_gather | solution.py:127
  277.5 116.4 %all-gather.26.cloned.1.call-start = ((), (), s32[]{:S(2)}) async-start(), calls=%async_computation.10 | async-start | bytes 2785280 | tf_op jit(solution)/shard_map/all_gather | solution.py:128
  278.1 215.7 %all-gather.34.cloned.1.call-start = ((), (), s32[]{:S(2)}) async-start(), calls=%async_computation.14 | async-start | bytes 19531776 | tf_op jit(solution)/shard_map/all_gather | solution.py:99
  282.3 385.2 %all-gather.36.cloned.1.call-start = ((), (), s32[]{:S(2)}) async-start(), calls=%async_computation.15 | async-start | bytes 19531776 | tf_op jit(solution)/shard_map/all_gather | solution.py:100
  286.5 831.1 %reduce-scatter.7.cloned.1.call-start = ((), (), s32[]{:S(2)}) async-start(), calls=%async_computation.5 | async-start | bytes 2785280 | tf_op jit(solution)/shard_map/reduce_scatter | solution.py:212
  849.4 17.7 slice-start.5
  849.4 17.7 slice-start.6
  887.7 229.8 %reduce-scatter.5.cloned.1.call-start = ((), (), s32[]{:S(2)}) async-start(), calls=%async_computation.4 | async-start | bytes 2785280 | tf_op jit(solution)/shard_map/reduce_scatter | solution.py:209
  902.5 16.3 copy-start.26
  921.8 206.3 %reduce-scatter.11.cloned.1.call-start = ((), (), s32[]{:S(2)}) async-start(), calls=%async_computation.7 | async-start | bytes 2785280 | tf_op jit(solution)/shard_map/reduce_scatter | solution.py:212
  968.9 24.6 %copy-start.10 = (f32[256,1088]{0,1:T(8,128)S(1)}, f32[256,1088]{0,1:T(8,128)}, u32[]{:S(2)}) copy-start(f32[256,1088]{0,1:T(8,128)} %get-tuple-element.73) | copy-start | bytes 3342340
  1008.9 119.2 %reduce-scatter.9.cloned.1.call-start = ((), (), s32[]{:S(2)}) async-start(), calls=%async_computation.6 | async-start | bytes 2785280 | tf_op jit(solution)/shard_map/reduce_scatter | solution.py:209
  1063.8 904.2 %all-reduce.9.cloned.1.call-start = ((), (), s32[]{:S(2)}) async-start(), calls=%async_computation.16 | async-start | bytes 113639424
  (65 other events, 307.5 us)
Sparse Core Ops, SparseCore 0:
  11.5 106.9 all-gather.29
  122.0 61.8 all-gather.31
  267.3 21.7 all-gather.23
  291.0 23.5 all-gather.21
  316.1 23.5 all-gather.27
  341.7 23.5 all-gather.25
  368.7 125.0 all-gather.33
  497.2 123.1 all-gather.35
  887.9 30.4 reduce-scatter.6
  921.9 31.1 reduce-scatter.4
  1009.0 31.3 reduce-scatter.10
  1063.9 31.1 reduce-scatter.8
  1155.7 812.2 all-reduce.8
where the time goes:
time: 2010 us; the launch traced here: 2000 us
  waiting for transfers between devices  888 us (44%)
  other arithmetic  545 us (27%)
  matrix products  273 us (14%)
  local copies, waits for them, and re-layouts  193 us (10%)
  blocking collectives  82.2 us (4%)
    unnamed x14, waiting for transfers between devices  737 us
    all_gather x1, other arithmetic, local(): lax.all_gather(shard_rows[3], ('dp', 'ctx'), axis=0, tiled=True)  156 us
    all_gather x1, other arithmetic, local(): lax.all_gather(shard_rows[2], ('dp', 'ctx'), axis=0, tiled=True)  156 us
    all_gather x1, other arithmetic, local(): lax.all_gather(shard_rows[0], ('dp', 'ctx'), axis=0, tiled=True)  130 us
    all_gather x1, waiting for transfers between devices, local(): lax.all_gather(shard_rows[2], ('dp', 'ctx'), axis=0, tiled=True)  88.8 us
    unnamed x2, blocking collectives  82.2 us
    dot_general x8, matrix products, lead_dot(): lax.dot_general(left_side, right_side, (((0,), (0,)), ((), ())), preferre...  74.7 us
    all_gather x1, waiting for transfers between devices, local(): lax.all_gather(shard_rows[0], ('dp', 'ctx'), axis=0, tiled=True)  62.4 us
  transfers between devices with their start and end apart: 13, of which 3 were waited for; matrix products, arithmetic and copies ran while one was open for 36% of the time, Pallas kernels for 0%

commit v1 on v0

v1 whole, which is shorter than its diff:
```python
import jax
import jax.numpy as jnp
from jax import lax
from jax.sharding import Mesh, PartitionSpec as P

HEADS = 17
HEAD_DIM = 64
FF = 4352
LANES = 8
SWAP = ((0, 1), (1, 0))
OWNERS = ("dp", "y")


def layer_stats(values):
    center = values - jnp.mean(values, axis=-1, keepdims=True)
    inverse = lax.rsqrt(jnp.mean(center * center, axis=-1, keepdims=True) + 1e-05)
    return (center * inverse, inverse)


def norm_back(upstream, normed, inverse, gain_vector):
    scaled = upstream * gain_vector
    return inverse * (
        scaled
        - jnp.mean(scaled, axis=-1, keepdims=True)
        - normed * jnp.mean(scaled * normed, axis=-1, keepdims=True)
    )


def lead_dot(left_side, right_side):
    return lax.dot_general(
        left_side, right_side, (((0,), (0,)), ((), ())), preferred_element_type=jnp.float32
    )


def tail_dot(left_side, right_side):
    return lax.dot_general(
        left_side, right_side, (((1,), (1,)), ((), ())), preferred_element_type=jnp.float32
    )


def smooth_gate(values):
    return jax.nn.gelu(values, approximate=True)


def pack_small(values, width):
    room = LANES * width - values.shape[-1]
    padded = jnp.pad(values, [(0, 0)] * (values.ndim - 1) + [(0, room)])
    return padded.reshape(values.shape[:-1] + (LANES, width))


def gather_packed(block, core):
    own = lax.all_gather(block, OWNERS, axis=0, tiled=True)
    other = lax.ppermute(own, "core", SWAP)
    even = jnp.where(core == 0, own, other)
    odd = jnp.where(core == 0, other, own)
    shape = (-1, 1, LANES, block.shape[1])
    return jnp.concatenate([even.reshape(shape), odd.reshape(shape)], axis=1)


def scatter_packed(packed, core):
    even, odd = packed[:, 0], packed[:, 1]
    keep = jnp.where(core == 0, even, odd)
    give = jnp.where(core == 0, odd, even)
    got = lax.ppermute(give, "core", SWAP)
    pair = (keep.astype(jnp.float32) + got.astype(jnp.float32)).astype(jnp.bfloat16)
    return lax.psum_scatter(pair, OWNERS, scatter_dimension=0, tiled=True)[0]


def local(tokens, positions, w_qkv, w_out, w_up, w_down, small_params, cotangent):
    seqs_here, local_len, model_width = tokens.shape
    seq_len = positions.shape[1]
    rows = seqs_here * local_len
    factor = HEAD_DIM ** (-0.5)
    y = lax.axis_index("y")
    core = lax.axis_index("core")
    pairs = lax.axis_size("dp") * 2
    small_len = small_params.shape[0]
    small_width = -(-small_len // LANES)
    qkv_width = w_qkv.shape[0] // LANES

    def trade(values):
        mine = lax.dynamic_index_in_dim(values, y, 0, keepdims=False)
        give = lax.dynamic_index_in_dim(values, 1 - y, 0, keepdims=False)
        return jnp.concatenate([mine, lax.ppermute(give, "y", SWAP)], axis=0)

    def trade_back(values):
        mine = values[:local_len]
        got = lax.ppermute(values[local_len:], "y", SWAP)
        first = jnp.where(y == 0, mine, got)
        second = jnp.where(y == 0, got, mine)
        return jnp.stack([first, second])

    first_block = jnp.concatenate(
        [w_qkv.reshape(LANES, qkv_width), pack_small(small_params, small_width)], axis=1
    )
    inputs = trade(tokens)
    qkv_small = gather_packed(first_block, core)
    out_mat = gather_packed(w_out.reshape(LANES, -1), core).reshape(model_width, model_width)
    up_mat = gather_packed(w_up.reshape(LANES, -1), core).reshape(model_width, FF)
    down_mat = gather_packed(w_down.reshape(LANES, -1), core).reshape(FF, model_width)
    grad_rows = trade(cotangent)

    qkv_mat = qkv_small[..., :qkv_width].reshape(model_width, 3 * model_width)
    packed = qkv_small[..., qkv_width:].reshape(2 * pairs, -1)[:, :small_len]
    packed = packed.reshape(-1).astype(jnp.float32)
    pieces = [packed[number * model_width : (number + 1) * model_width] for number in range(7)]
    gain_one, bias_one, bias_query, bias_value, bias_out, gain_two, bias_two = pieces
    up_bias = packed[7 * model_width : 7 * model_width + FF]
    down_bias = packed[7 * model_width + FF :]

    place_row = lax.dynamic_index_in_dim(positions, y, 0, keepdims=False)

    def places_of(core_index):
        near = lax.dynamic_slice_in_dim(place_row, (2 * y + core_index) * local_len, local_len)
        far = lax.dynamic_slice_in_dim(place_row, (2 - 2 * y + core_index) * local_len, local_len)
        return jnp.concatenate([near, far])

    places = places_of(core)
    key_places = jnp.concatenate([places, places_of(1 - core)])
    allowed = (key_places[None, :] <= places[:, None])[None]

    inputs = inputs.astype(jnp.float32)
    normed_one, inverse_one = layer_stats(inputs)
    act_one = (normed_one * gain_one + bias_one).astype(jnp.bfloat16)
    qkv_bias = jnp.concatenate([bias_query, jnp.zeros_like(bias_query), bias_value])
    qkv_rows = (jnp.dot(act_one, qkv_mat, preferred_element_type=jnp.float32) + qkv_bias).astype(
        jnp.bfloat16
    )
    kv_all = jnp.concatenate(
        [qkv_rows[:, model_width:], lax.ppermute(qkv_rows[:, model_width:], "core", SWAP)], axis=0
    )
    query = qkv_rows[:, :model_width].reshape(rows, HEADS, HEAD_DIM)
    keys = kv_all[:, :model_width].reshape(seq_len, HEADS, HEAD_DIM)
    vals = kv_all[:, model_width:].reshape(seq_len, HEADS, HEAD_DIM)

    def masked_scores():
        scores = jnp.einsum("qhd,khd->hqk", query, keys, preferred_element_type=jnp.float32)
        return jnp.where(allowed, scores * factor, -1e30)

    scores = masked_scores()
    top_score = jnp.max(scores, axis=-1, keepdims=True)
    expo = jnp.exp(scores - top_score)
    denom = jnp.sum(expo, axis=-1, keepdims=True)
    probs = expo / denom
    log_total = top_score + jnp.log(denom)
    mixed = jnp.einsum(
        "hqk,khd->qhd", probs.astype(jnp.bfloat16), vals, preferred_element_type=jnp.float32
    )
    mixed = mixed.astype(jnp.bfloat16).reshape(rows, model_width)
    resid = inputs + jnp.dot(mixed, out_mat, preferred_element_type=jnp.float32) + bias_out
    normed_two, inverse_two = layer_stats(resid)
    act_two = (normed_two * gain_two + bias_two).astype(jnp.bfloat16)
    pre_act = jnp.dot(act_two, up_mat, preferred_element_type=jnp.float32) + up_bias
    gelu_rows = smooth_gate(pre_act).astype(jnp.bfloat16)
    outputs = resid + jnp.dot(gelu_rows, down_mat, preferred_element_type=jnp.float32) + down_bias
    result = trade_back(outputs.astype(jnp.bfloat16))

    def send_sum(grad, extra=None):
        grad = grad.astype(jnp.bfloat16).reshape(pairs, 2, LANES, -1)
        if extra is not None:
            grad = jnp.concatenate([grad, extra], axis=-1)
        return scatter_packed(grad, core)

    grad_float = grad_rows.astype(jnp.float32)
    sum_down = send_sum(lead_dot(gelu_rows, grad_rows))
    down_bias_term = jnp.sum(grad_float, axis=0)
    grad_gelu = tail_dot(grad_rows, down_mat)
    gelu_pull = jax.vjp(smooth_gate, pre_act)[1]
    grad_pre = gelu_pull(grad_gelu)[0].astype(jnp.bfloat16)
    sum_up = send_sum(lead_dot(act_two, grad_pre))
    up_bias_term = jnp.sum(grad_pre.astype(jnp.float32), axis=0)
    grad_act_two = tail_dot(grad_pre, up_mat)
    gain_two_term = jnp.sum(grad_act_two * normed_two, axis=0)
    bias_two_term = jnp.sum(grad_act_two, axis=0)
    grad_resid = grad_float + norm_back(grad_act_two, normed_two, inverse_two, gain_two)
    grad_attn = grad_resid.astype(jnp.bfloat16)
    sum_out = send_sum(lead_dot(mixed, grad_attn))
    bias_out_term = jnp.sum(grad_attn.astype(jnp.float32), axis=0)
    grad_mixed = tail_dot(grad_attn, out_mat).astype(jnp.bfloat16)
    grad_mixed = grad_mixed.reshape(rows, HEADS, HEAD_DIM)
    probs_again = jnp.exp(masked_scores() - log_total)
    grad_probs = jnp.einsum("qhd,khd->hqk", grad_mixed, vals, preferred_element_type=jnp.float32)
    grad_scores = probs_again * (
        grad_probs - jnp.sum(grad_probs * probs_again, axis=-1, keepdims=True)
    )
    grad_scores = grad_scores.astype(jnp.bfloat16)
    grad_query = (
        jnp.einsum("hqk,khd->qhd", grad_scores, keys, preferred_element_type=jnp.float32) * factor
    )
    key_terms = (
        jnp.einsum("hqk,qhd->khd", grad_scores, query, preferred_element_type=jnp.float32) * factor
    )
    value_terms = jnp.einsum(
        "hqk,qhd->khd",
        probs_again.astype(jnp.bfloat16),
        grad_mixed,
        preferred_element_type=jnp.float32,
    )
    kv_terms = jnp.concatenate(
        [key_terms.reshape(seq_len, model_width), value_terms.reshape(seq_len, model_width)], axis=1
    )
    kv_got = lax.ppermute(kv_terms[rows:].astype(jnp.bfloat16), "core", SWAP)
    grad_kv = kv_terms[:rows] + kv_got.astype(jnp.float32)
    grad_qkv_rows = jnp.concatenate(
        [grad_query.reshape(rows, model_width), grad_kv], axis=1
    ).astype(jnp.bfloat16)
    qkv_sums = jnp.sum(grad_qkv_rows.astype(jnp.float32), axis=0)
    grad_act_one = tail_dot(grad_qkv_rows, qkv_mat)
    gain_one_term = jnp.sum(grad_act_one * normed_one, axis=0)
    bias_one_term = jnp.sum(grad_act_one, axis=0)
    small_grad = jnp.concatenate(
        [
            gain_one_term,
            bias_one_term,
            qkv_sums[:model_width],
            qkv_sums[2 * model_width :],
            bias_out_term,
            gain_two_term,
            bias_two_term,
            up_bias_term,
            down_bias_term,
        ]
    ).astype(jnp.bfloat16)
    small_grad = pack_small(small_grad.reshape(pairs, 2, small_len), small_width)
    sum_qkv = send_sum(lead_dot(act_one, grad_qkv_rows), small_grad)
    grad_input = grad_resid + norm_back(grad_act_one, normed_one, inverse_one, gain_one)
    grad_tokens = trade_back(grad_input.astype(jnp.bfloat16))
    grad_qkv = sum_qkv[:, :qkv_width].astype(jnp.float32).reshape(-1)
    grad_small = sum_qkv[:, qkv_width:].astype(jnp.float32).reshape(-1)[:small_len]
    grad_out, grad_up, grad_down = [
        piece.astype(jnp.float32).reshape(-1) for piece in (sum_out, sum_up, sum_down)
    ]
    return (result, grad_tokens, grad_qkv, grad_out, grad_up, grad_down, grad_small)


def solution(mesh):
    groups, owners = mesh.shape["dp"], mesh.shape["ctx"]
    fine = Mesh(mesh.devices.reshape(groups, owners // 2, 2), ("dp", "y", "core"))
    rows = P("dp", ("y", "core"), None)
    flat = P(("dp", "y", "core"))
    return jax.shard_map(
        local,
        mesh=fine,
        in_specs=(rows, P("dp", None), flat, flat, flat, flat, flat, rows),
        out_specs=(rows, rows, flat, flat, flat, flat, flat),
        check_vma=False,
    )
```

time: 2010 us -> 1150 us (0.57)
  other arithmetic: 545 us -> 154 us
  waiting for transfers between devices: 888 us -> 537 us
  blocking collectives: 82.2 us -> 0 us
  matrix products: 273 us -> 199 us
  local copies, waits for them, and re-layouts: 193 us -> 226 us
    all_gather x4 -> x0, other arithmetic: 491 us -> none  [the longest x1 156 us: local(): lax.all_gather(shard_rows[3], ('dp', 'ctx'), axis=0, tiled=True)]
    unnamed x14 -> x12, waiting for transfers between devices: 737 us -> 251 us
    unnamed x2 -> x0, blocking collectives: 82.2 us -> none
    ppermute x0 -> x14, waiting for transfers between devices: none -> 81.9 us  [the longest x2 63.2 us: trade_back(): got = lax.ppermute(values[local_len:], 'y', SWAP)]
    all_gather x8 -> x4, waiting for transfers between devices: 151 us -> 204 us  [gather_packed(): own = lax.all_gather(block, OWNERS, axis=0, tiled=True)]
    dot_general x8 -> x4, matrix products: 74.7 us -> 31.3 us  [lead_dot(): lax.dot_general(left_side, right_side, (((0,), (0,)), ((), ())), preferre...]
    convert_element_type x1 -> x6, other arithmetic: 0.73 us -> 28.1 us  [the longest x4 24.8 us: scatter_packed(): (keep.astype(jnp.float32) + got.astype(jnp.float32)).astype(jnp.bfloat16)]
    unnamed x159 -> x120, local copies, waits for them, and re-layouts: 30.1 us -> 4.98 us
  transfers between devices with their start and end apart: 13 -> 22, of which waited for: 3 -> 11; matrix products, arithmetic and copies ran while one was open for 36% -> 30% of each run, Pallas kernels for 0% -> 0%
where the time goes in v1:
time: 1150 us; the launch traced here: 1140 us
  waiting for transfers between devices  537 us (47%)
  local copies, waits for them, and re-layouts  226 us (20%)
  matrix products  199 us (17%)
  other arithmetic  154 us (13%)
  between operations  15.4 us (1%)
    unnamed x12, waiting for transfers between devices  251 us
    all_gather x4, waiting for transfers between devices, gather_packed(): own = lax.all_gather(block, OWNERS, axis=0, tiled=True)  204 us
    ppermute x2, waiting for transfers between devices, trade_back(): got = lax.ppermute(values[local_len:], 'y', SWAP)  63.2 us
    reshape x4, local copies, waits for them, and re-layouts, send_sum(): grad = grad.astype(jnp.bfloat16).reshape(pairs, 2, LANES, -1)  58.8 us
    dot_general x4, matrix products, tail_dot(): lax.dot_general(left_side, right_side, (((1,), (1,)), ((), ())), preferre...  35.7 us
    dot_general x4, matrix products, lead_dot(): lax.dot_general(left_side, right_side, (((0,), (0,)), ((), ())), preferre...  31.3 us
    convert_element_type x1, other arithmetic, local(): grad_scores = grad_scores.astype(jnp.bfloat16)  29.8 us
    dot_general x1, matrix products, local(): jnp.einsum('qhd,khd->hqk', grad_mixed, vals, preferred_element_type=jnp.f...  26.7 us
  transfers between devices with their start and end apart: 22, of which 11 were waited for; matrix products, arithmetic and copies ran while one was open for 30% of the time, Pallas kernels for 0%

profile of v1, /device:TPU:0, one launch (start us, length us, event | category | flops | bytes accessed | tf_op | source)
XLA Modules:
  0.0 1139.3 jit_solution(9316874566011230910)
XLA Ops:
  13.8 71.4 %all-gather.5.cloned.1.call-done = bf16[128,13923]{1,0:T(8,128)(2,1)} async-done(((bf16[8,13923]{1,0:T(8,128)(2,1)}), bf16[128,13923]{1,0:T(8,128)(2,1)}) %all-gather.5.cloned.1.call-update) | async-done | bytes 3564304 | tf_op jit(solution)/shard_map/all_gather | solution.py:52
  108.9 34.7 %all-gather.7.cloned.1.call-done = bf16[128,4624]{1,0:T(8,128)(2,1)} async-done(((bf16[8,4624]{1,0:T(8,128)(2,1)}), bf16[128,4624]{1,0:T(8,128)(2,1)}) %all-gather.7.cloned.1.call-update) | async-done | bytes 1183760 | tf_op jit(solution)/shard_map/all_gather | solution.py:52
  166.0 15.3 %reshape.251 = bf16[1088,3264]{1,0:T(8,128)(2,1)} reshape(bf16[16,2,8,13872]{3,2,1,0:T(8,128)(2,1)} %copy.64) | data formatting | bytes 14204928 | tf_op jit(solution)/shard_map/reshape | solution.py:103
  203.4 22.9 %all-gather.9.cloned.1.call-done = bf16[128,18496]{1,0:T(8,128)(2,1)} async-done(((bf16[8,18496]{1,0:T(8,128)(2,1)}), bf16[128,18496]{1,0:T(8,128)(2,1)}) %all-gather.9.cloned.1.call-update) | async-done | bytes 4734992 | tf_op jit(solution)/shard_map/all_gather | solution.py:52
  233.8 74.8 %all-gather.11.cloned.1.call-done = bf16[128,18496]{1,0:T(8,128)(2,1)} async-done(((bf16[8,18496]{1,0:T(8,128)(2,1)}), bf16[128,18496]{1,0:T(8,128)(2,1)}) %all-gather.11.cloned.1.call-update) | async-done | bytes 4734992 | tf_op jit(solution)/shard_map/all_gather | solution.py:52
  322.0 14.8 %fusion.6 = (f32[17,512]{1,0:T(8,128)S(1)}, f32[17,512,1024]{2,1,0:T(8,128)}) fusion(pred[512,1024]{1,0:T(8,128)(4,1)S(1)} %broadcast_compare_fusion, bf16[512,17,64]{0,2,1:T(8,128)(2,1)S(1)} %bitcast.164, bf16[1024,17,64]{0,2,1:T(8,128)(2,1)S(1)} %bitcast.162), kind=kOutput, calls=%fused_computation.14 | convolution fusion | flops 1167580672 | bytes 39553024 | tf_op jit(solution)/shard_map/qhd,khd->hqk/dot_general | solution.py:137
  336.8 15.7 %fusion = f32[17,512]{1,0:T(8,128)S(1)} fusion(f32[17,512]{1,0:T(8,128)S(1)} %get-tuple-element.50, f32[17,512,1024]{2,1,0:T(8,128)} %get-tuple-element.51, pred[512,1024]{1,0:T(8,128)(4,1)S(1)} %broadcast_compare_fusion), kind=kLoop, calls=%fused_computation.6 | loop fusion | flops 35642880 | bytes 36245504 | tf_op jit(solution)/shard_map/reduce_sum | solution.py:143
  352.6 15.2 %fusion.46 = bf16[17,64,512]{2,1,0:T(8,128)(2,1)S(1)} fusion(bf16[1024,17,64]{0,2,1:T(8,128)(2,1)S(1)} %bitcast.168, f32[17,512]{1,0:T(8,128)S(1)} %fusion, f32[17,512]{1,0:T(8,128)S(1)} %get-tuple-element.50, f32[17,512,1024]{2,1,0:T(8,128)} %get-tuple-element.51, pred[512,1024]{1,0:T(8,128)(4,1)S(1)} %broadcast_compare_fusion), kind=kOutput, calls=%fused_computation.104 | convolution fusion | flops 1185972224 | bytes 39587840 | tf_op jit(solution)/shard_map/hqk,khd->qhd/dot_general | solution.py:146
  402.7 16.4 %reshape.263 = bf16[1088,4352]{1,0:T(8,128)(2,1)} reshape(bf16[16,2,8,18496]{3,2,1,0:T(8,128)(2,1)} %copy.72) | data formatting | bytes 18939904 | tf_op jit(solution)/shard_map/reshape | solution.py:99
  451.4 18.3 %reshape.267 = bf16[4352,1088]{1,0:T(8,128)(2,1)} reshape(bf16[16,2,8,18496]{3,2,1,0:T(8,128)(2,1)} %copy.76) | data formatting | bytes 18939904 | tf_op jit(solution)/shard_map/reshape | solution.py:100
  482.2 15.6 %fusion.67 = (bf16[4352]{0:T(1024)(128)(2,1)S(1)}, bf16[512,4352]{1,0:T(8,128)(2,1)}) fusion(f32[512,4352]{1,0:T(8,128)} %fusion.62, f32[4352]{0:T(1024)S(1)} %copy-done.45, bf16[4352,1088]{1,0:T(8,128)(2,1)} %reshape.267, bf16[256,1088]{0,1:T(8,128)(2,1)S(1)} %copy-done.29, bf16[256,1088]{0,1:T(8,128)(2,1)S(1)} %copy-done.27), kind=kOutput, calls=%fused_computation.158 | convolution fusion | flops 4899860480 | bytes 23979520 | tf_op jit(solution)/shard_map/dot_general | solution.py:36
  513.9 18.5 %fusion.2 = f32[17,64,1024]{2,1,0:T(8,128)} fusion(bf16[512,17,64]{0,2,1:T(8,128)(2,1)} %bitcast.173, f32[17,512]{1,0:T(8,128)S(1)} %log_add_fusion, f32[17,512,1024]{2,1,0:T(8,128)} %get-tuple-element.51, pred[512,1024]{1,0:T(8,128)(4,1)S(1)} %broadcast_compare_fusion), kind=kOutput, calls=%fused_computation.10 | convolution fusion | flops 1176502272 | bytes 41781248 | tf_op jit(solution)/shard_map/hqk,qhd->khd/dot_general | solution.py:193
  532.5 26.7 %multiply_reduce_fusion = (f32[17,512]{1,0:T(8,128)S(1)}, f32[17,512,1024]{2,1,0:T(8,128)}) fusion(f32[17,512]{1,0:T(8,128)S(1)} %log_add_fusion, f32[17,512,1024]{2,1,0:T(8,128)} %get-tuple-element.51, pred[512,1024]{1,0:T(8,128)(4,1)S(1)} %broadcast_compare_fusion, bf16[512,17,64]{0,2,1:T(8,128)(2,1)} %bitcast.174, bf16[1024,17,64]{0,2,1:T(8,128)(2,1)S(1)} %bitcast.169), kind=kOutput, calls=%fused_computation.1 | convolution fusion | flops 1185406464 | bytes 75239424 | tf_op jit(solution)/shard_map/qhd,khd->hqk/dot_general | solution.py:182
  569.5 13.9 %copy.83 = bf16[4352,1088]{1,0:T(8,128)(2,1)} copy(bf16[4352,1088]{0,1:T(8,128)(2,1)} %convolution_convert_fusion) | data formatting | bytes 18939904 | tf_op jit(solution)/shard_map/convert_element_type | solution.py:159
  583.4 19.5 %reshape.277 = bf16[16,2,8,18496]{3,2,1,0:T(8,128)(2,1)} reshape(bf16[4352,1088]{1,0:T(8,128)(2,1)} %copy.83) | data formatting | bytes 18939904 | tf_op jit(solution)/shard_map/reshape | solution.py:159
  608.6 29.8 %multiply_convert_fusion = bf16[17,512,1024]{2,1,0:T(8,128)(2,1)} fusion(f32[17,512,1024]{2,1,0:T(8,128)} %get-tuple-element.56, f32[17,512]{1,0:T(8,128)S(1)} %get-tuple-element.55, f32[17,512]{1,0:T(8,128)S(1)} %log_add_fusion, f32[17,512,1024]{2,1,0:T(8,128)} %get-tuple-element.51, pred[512,1024]{1,0:T(8,128)(4,1)S(1)} %broadcast_compare_fusion), kind=kLoop, calls=%fused_computation | loop fusion | flops 53477376 | bytes 89722880 | tf_op jit(solution)/shard_map/convert_element_type | solution.py:186
  688.5 16.3 %reshape.272 = bf16[16,2,8,13872]{3,2,1,0:T(8,128)(2,1)} reshape(bf16[1088,3264]{1,0:T(8,128)(2,1)} %convolution_convert_fusion.2) | data formatting | bytes 14204928 | tf_op jit(solution)/shard_map/reshape | solution.py:159
  738.9 17.4 %reshape.276 = bf16[16,2,8,18496]{3,2,1,0:T(8,128)(2,1)} reshape(bf16[1088,4352]{1,0:T(8,128)(2,1)} %convolution_convert_fusion.1) | data formatting | bytes 18939904 | tf_op jit(solution)/shard_map/reshape | solution.py:159
  786.4 13.2 %fusion.28 = bf16[512,1088]{0,1:T(8,128)(2,1)} fusion(f32[512,1088]{0,1:T(8,128)S(1)} %copy-done.8, bf16[4352,1088]{1,0:T(8,128)(2,1)} %reshape.267, f32[1088]{0:T(1024)S(1)} %copy-done.51, f32[512,4352]{1,0:T(8,128)} %fusion.62, f32[4352]{0:T(1024)S(1)} %copy-done.45), kind=kOutput, calls=%fused_computation.73 | convolution fusion | flops 4872568832 | bytes 21746944 | tf_op jit(solution)/shard_map/dot_general | solution.py:155
  806.0 28.7 %collective-permute-done.6 = bf16[256,1088]{0,1:T(8,128)(2,1)S(1)} collective-permute-done((bf16[256,1088]{0,1:T(8,128)(2,1)S(1)}, bf16[256,1088]{0,1:T(8,128)(2,1)S(1)}, u32[]{:S(2)}, u32[]{:S(2)}) %collective-permute-start.6) | collective-permute-done | bytes 557088 | tf_op jit(solution)/shard_map/ppermute | solution.py:88
  835.9 34.5 %collective-permute-done.9 = bf16[256,1088]{0,1:T(8,128)(2,1)S(1)} collective-permute-done((bf16[256,1088]{0,1:T(8,128)(2,1)S(1)}, bf16[256,1088]{0,1:T(8,128)(2,1)S(1)}, u32[]{:S(2)}, u32[]{:S(2)}) %collective-permute-start.9) | collective-permute-done | bytes 557088 | tf_op jit(solution)/shard_map/ppermute | solution.py:88
  873.2 31.2 %reduce-scatter.17.cloned.1.call-done = bf16[1,8,13923]{2,1,0:T(8,128)(2,1)} async-done(((bf16[16,8,13923]{2,1,0:T(8,128)(2,1)}), bf16[1,8,13923]{2,1,0:T(8,128)(2,1)}) %reduce-scatter.17.cloned.1.call-update) | async-done | bytes 222784
  907.8 111.4 %reduce-scatter.23.cloned.1.call-done = bf16[1,8,18496]{2,1,0:T(8,128)(2,1)} async-done(((bf16[16,8,18496]{2,1,0:T(8,128)(2,1)}), bf16[1,8,18496]{2,1,0:T(8,128)(2,1)}) %reduce-scatter.23.cloned.1.call-update) | async-done | bytes 295952
  1021.3 108.7 %reduce-scatter.21.cloned.1.call-done = bf16[1,8,18496]{2,1,0:T(8,128)(2,1)} async-done(((bf16[16,8,18496]{2,1,0:T(8,128)(2,1)}), bf16[1,8,18496]{2,1,0:T(8,128)(2,1)}) %reduce-scatter.21.cloned.1.call-update) | async-done | bytes 295952
  (262 shorter events, 339.1 us)
Async XLA Ops:
  7.2 78.1 %all-gather.5.cloned.1.call-start = ((), (), s32[]{:S(2)}) async-start(), calls=%async_computation.4 | async-start | bytes 3794944 | tf_op jit(solution)/shard_map/all_gather | solution.py:52
  10.0 133.6 %all-gather.7.cloned.1.call-start = ((), (), s32[]{:S(2)}) async-start(), calls=%async_computation.5 | async-start | bytes 1288192 | tf_op jit(solution)/shard_map/all_gather | solution.py:52
  11.7 214.6 %all-gather.9.cloned.1.call-start = ((), (), s32[]{:S(2)}) async-start(), calls=%async_computation.6 | async-start | bytes 5048320 | tf_op jit(solution)/shard_map/all_gather | solution.py:52
  13.8 294.8 %all-gather.11.cloned.1.call-start = ((), (), s32[]{:S(2)}) async-start(), calls=%async_computation.7 | async-start | bytes 5048320 | tf_op jit(solution)/shard_map/all_gather | solution.py:52
  91.2 54.8 %collective-permute-start.1 = (bf16[128,13923]{0,1:T(8,128)(2,1)}, bf16[128,13923]{0,1:T(8,128)(2,1)}, u32[]{:S(2)}, u32[]{:S(2)}) collective-permute-start(bf16[128,13923]{0,1:T(8,128)(2,1)} %copy.60), channel_id=1, source_target_pairs={{0,1},{1,0},{2,3},{3,2},{4,5},{5,4},{6,7},{7,6},{8,9},{9,8},{10,11... | collective-permute-start | bytes 10692872 | tf_op jit(solution)/shard_map/ppermute | solution.py:53
  92.1 275.7 %copy-start.13 = (bf16[256,1088]{0,1:T(8,128)(2,1)}, bf16[256,1088]{0,1:T(8,128)(2,1)S(1)}, u32[]{:S(2)}) copy-start(bf16[256,1088]{0,1:T(8,128)(2,1)S(1)} %get-tuple-element.34) | copy-start | bytes 1671172
  92.1 16.2 %collective-permute-start = (bf16[256,1088]{0,1:T(8,128)(2,1)}, bf16[256,1088]{0,1:T(8,128)(2,1)S(1)}, u32[]{:S(2)}, u32[]{:S(2)}) collective-permute-start(bf16[256,1088]{0,1:T(8,128)(2,1)} %get-tuple-element.35), channel_id=1, source_target_pairs={{0,2},{2,0},{1,3},{3,1},{4,6},{6,4},{5,7},{7,5},{8,10},{10,8},{9,1... | collective-permute-start | bytes 1671176 | tf_op jit(solution)/shard_map/ppermute | solution.py:84
  94.6 98.8 %collective-permute-start.7 = (bf16[256,1088]{0,1:T(8,128)(2,1)S(1)}, bf16[256,1088]{0,1:T(8,128)(2,1)S(1)}, u32[]{:S(2)}, u32[]{:S(2)}) collective-permute-start(bf16[256,1088]{0,1:T(8,128)(2,1)S(1)} %get-tuple-element.32), channel_id=1, source_target_pairs={{0,2},{2,0},{1,3},{3,1},{4,6},{6,4},{5,7},{7,5},{8,10},{10,8},{9,1... | collective-permute-start | bytes 1671176 | tf_op jit(solution)/shard_map/ppermute | solution.py:84
  97.1 774.4 %reduce-scatter.19.cloned.1.call-start = ((), (), s32[]{:S(2)}) async-start(), calls=%async_computation.9 | async-start | bytes 1288192
  146.0 48.3 %collective-permute-start.3 = (bf16[128,4624]{0,1:T(8,128)(2,1)}, bf16[128,4624]{0,1:T(8,128)(2,1)}, u32[]{:S(2)}, u32[]{:S(2)}) collective-permute-start(bf16[128,4624]{0,1:T(8,128)(2,1)} %copy.65), channel_id=1, source_target_pairs={{0,1},{1,0},{2,3},{3,2},{4,5},{5,4},{6,7},{7,6},{8,9},{9,8},{10,11... | collective-permute-start | bytes 3551240 | tf_op jit(solution)/shard_map/ppermute | solution.py:53
  192.1 126.7 %collective-permute-start.2 = (bf16[512,2176]{0,1:T(8,128)(2,1)}, bf16[512,2176]{0,1:T(8,128)(2,1)}, u32[]{:S(2)}, u32[]{:S(2)}) collective-permute-start(bf16[512,2176]{0,1:T(8,128)(2,1)} %slice.140), channel_id=1, source_target_pairs={{0,1},{1,0},{2,3},{3,2},{4,5},{5,4},{6,7},{7,6},{8,9},{9,8},{10,11... | collective-permute-start | bytes 6684680 | tf_op jit(solution)/shard_map/ppermute | solution.py:130
  233.8 136.2 %collective-permute-start.4 = (bf16[128,18496]{0,1:T(8,128)(2,1)}, bf16[128,18496]{0,1:T(8,128)(2,1)}, u32[]{:S(2)}, u32[]{:S(2)}) collective-permute-start(bf16[128,18496]{0,1:T(8,128)(2,1)} %copy.69), channel_id=1, source_target_pairs={{0,1},{1,0},{2,3},{3,2},{4,5},{5,4},{6,7},{7,6},{8,9},{9,8},{10,11... | collective-permute-start | bytes 14204936 | tf_op jit(solution)/shard_map/ppermute | solution.py:53
  316.0 103.1 %collective-permute-start.5 = (bf16[128,18496]{0,1:T(8,128)(2,1)}, bf16[128,18496]{0,1:T(8,128)(2,1)}, u32[]{:S(2)}, u32[]{:S(2)}) collective-permute-start(bf16[128,18496]{0,1:T(8,128)(2,1)} %copy.73), channel_id=1, source_target_pairs={{0,1},{1,0},{2,3},{3,2},{4,5},{5,4},{6,7},{7,6},{8,9},{9,8},{10,11... | collective-permute-start | bytes 14204936 | tf_op jit(solution)/shard_map/ppermute | solution.py:53
  369.6 136.9 %copy-start.6 = (f32[512,1088]{0,1:T(8,128)}, f32[512,1088]{0,1:T(8,128)S(1)}, u32[]{:S(2)}) copy-start(f32[512,1088]{0,1:T(8,128)S(1)} %get-tuple-element.53) | copy-start | bytes 6684676
  652.7 14.3 %collective-permute-start.8 = (bf16[512,2176]{0,1:T(8,128)(2,1)}, bf16[512,2176]{0,1:T(8,128)(2,1)}, u32[]{:S(2)}, u32[]{:S(2)}) collective-permute-start(bf16[512,2176]{0,1:T(8,128)(2,1)} %fusion.22), channel_id=1, source_target_pairs={{0,1},{1,0},{2,3},{3,2},{4,5},{5,4},{6,7},{7,6},{8,9},{9,8},{10,11... | collective-permute-start | bytes 6684680 | tf_op jit(solution)/shard_map/ppermute | solution.py:202
  654.4 63.5 %collective-permute-start.11 = (bf16[16,8,4624]{2,1,0:T(8,128)(2,1)}, bf16[16,8,4624]{2,1,0:T(8,128)(2,1)}, u32[]{:S(2)}, u32[]{:S(2)}) collective-permute-start(bf16[16,8,4624]{2,1,0:T(8,128)(2,1)} %select_bitcast_fusion.8), channel_id=1, source_target_pairs={{0,1},{1,0},{2,3},{3,2},{4,5},{5,4},{6,7},{7,6},{8,9},{9,8},{10,11... | collective-permute-start | bytes 3551240 | tf_op jit(solution)/shard_map/ppermute | solution.py:64
  710.3 10.4 collective-permute-start.10
  717.7 38.6 %collective-permute-start.13 = (bf16[16,8,18496]{2,1,0:T(8,128)(2,1)}, bf16[16,8,18496]{2,1,0:T(8,128)(2,1)}, u32[]{:S(2)}, u32[]{:S(2)}) collective-permute-start(bf16[16,8,18496]{2,1,0:T(8,128)(2,1)} %fusion.17), channel_id=1, source_target_pairs={{0,1},{1,0},{2,3},{3,2},{4,5},{5,4},{6,7},{7,6},{8,9},{9,8},{10,11... | collective-permute-start | bytes 14204936 | tf_op jit(solution)/shard_map/ppermute | solution.py:64
  720.6 183.8 %reduce-scatter.17.cloned.1.call-start = ((), (), s32[]{:S(2)}) async-start(), calls=%async_computation.8 | async-start | bytes 3794944
  727.3 292.0 %reduce-scatter.23.cloned.1.call-start = ((), (), s32[]{:S(2)}) async-start(), calls=%async_computation.11 | async-start | bytes 5048320
  765.4 364.6 %reduce-scatter.21.cloned.1.call-start = ((), (), s32[]{:S(2)}) async-start(), calls=%async_computation.10 | async-start | bytes 5048320
  770.2 8.2 collective-permute-start.12
  800.6 34.0 %collective-permute-start.6 = (bf16[256,1088]{0,1:T(8,128)(2,1)S(1)}, bf16[256,1088]{0,1:T(8,128)(2,1)S(1)}, u32[]{:S(2)}, u32[]{:S(2)}) collective-permute-start(bf16[256,1088]{0,1:T(8,128)(2,1)S(1)} %slice.150), channel_id=1, source_target_pairs={{0,2},{2,0},{1,3},{3,1},{4,6},{6,4},{5,7},{7,5},{8,10},{10,8},{9,1... | collective-permute-start | bytes 1671176 | tf_op jit(solution)/shard_map/ppermute | solution.py:88
  805.5 64.9 %collective-permute-start.9 = (bf16[256,1088]{0,1:T(8,128)(2,1)S(1)}, bf16[256,1088]{0,1:T(8,128)(2,1)S(1)}, u32[]{:S(2)}, u32[]{:S(2)}) collective-permute-start(bf16[256,1088]{0,1:T(8,128)(2,1)S(1)} %slice.154), channel_id=1, source_target_pairs={{0,2},{2,0},{1,3},{3,1},{4,6},{6,4},{5,7},{7,5},{8,10},{10,8},{9,1... | collective-permute-start | bytes 1671176 | tf_op jit(solution)/shard_map/ppermute | solution.py:88
  (58 other events, 1159.4 us)
Sparse Core Ops, SparseCore 0:
  11.3 73.9 all-gather.4
  88.5 55.0 all-gather.6
  146.9 79.3 all-gather.8
  229.4 79.0 all-gather.10
  720.8 78.7 reduce-scatter.18
  801.8 102.5 reduce-scatter.16
  906.7 112.5 reduce-scatter.22
  1021.7 108.2 reduce-scatter.20

commit v2 on v1

v2 whole, which is shorter than its diff:
```python
import jax
import jax.numpy as jnp
from jax import lax
from jax.experimental import pallas as pl
from jax.experimental.pallas import tpu as pltpu
from jax.sharding import Mesh, PartitionSpec as P

HEADS = 17
HEAD_DIM = 64
FF = 4352
LANES = 8
SWAP = ((0, 1), (1, 0))
OWNERS = ("dp", "y")


def layer_stats(values):
    center = values - jnp.mean(values, axis=-1, keepdims=True)
    inverse = lax.rsqrt(jnp.mean(center * center, axis=-1, keepdims=True) + 1e-05)
    return (center * inverse, inverse)


def norm_back(upstream, normed, inverse, gain_vector):
    scaled = upstream * gain_vector
    return inverse * (
        scaled
        - jnp.mean(scaled, axis=-1, keepdims=True)
        - normed * jnp.mean(scaled * normed, axis=-1, keepdims=True)
    )


def lead_dot(left_side, right_side):
    return lax.dot_general(
        left_side, right_side, (((0,), (0,)), ((), ())), preferred_element_type=jnp.float32
    )


def tail_dot(left_side, right_side):
    return lax.dot_general(
        left_side, right_side, (((1,), (1,)), ((), ())), preferred_element_type=jnp.float32
    )


def smooth_gate(values):
    return jax.nn.gelu(values, approximate=True)


def pack_small(values, width):
    room = LANES * width - values.shape[-1]
    padded = jnp.pad(values, [(0, 0)] * (values.ndim - 1) + [(0, room)])
    return padded.reshape(values.shape[:-1] + (LANES, width))


def gather_packed(block, core):
    own = lax.all_gather(block, OWNERS, axis=0, tiled=True)
    other = lax.ppermute(own, "core", SWAP)
    even = jnp.where(core == 0, own, other)
    odd = jnp.where(core == 0, other, own)
    shape = (-1, 1, LANES, block.shape[1])
    return jnp.concatenate([even.reshape(shape), odd.reshape(shape)], axis=1)


def scatter_packed(packed, core):
    even, odd = packed[:, 0], packed[:, 1]
    keep = jnp.where(core == 0, even, odd)
    give = jnp.where(core == 0, odd, even)
    got = lax.ppermute(give, "core", SWAP)
    pair = (keep.astype(jnp.float32) + got.astype(jnp.float32)).astype(jnp.bfloat16)
    return lax.psum_scatter(pair, OWNERS, scatter_dimension=0, tiled=True)[0]


def dot_rows(left, right):
    return lax.dot_general(
        left, right, (((1,), (0,)), ((), ())), preferred_element_type=jnp.float32
    )


def bias_of(key_places, query_places):
    return jnp.where(key_places <= query_places, 0.0, -1e30).astype(jnp.float32)


def per_pair(one_pair):
    wide = 2 * HEAD_DIM
    full = HEADS // 2

    def step(number, carry):
        one_pair(pl.ds(pl.multiple_of(number * wide, wide), wide), 2 * number, 2)
        return carry

    lax.fori_loop(0, full, step, 0)
    if HEADS % 2:
        one_pair(pl.ds(full * wide, HEAD_DIM), 2 * full, 1)


def only_head(values, number, heads):
    if heads == 1:
        return values
    lane = lax.broadcasted_iota(jnp.int32, values.shape, 1)
    inside = lane < HEAD_DIM if number == 0 else lane >= HEAD_DIM
    return jnp.where(inside, values, jnp.zeros_like(values))


def join_heads(parts):
    if len(parts) == 1:
        return parts[0]
    lane = lax.broadcasted_iota(jnp.int32, parts[0].shape, 1)
    return jnp.where(lane < HEAD_DIM, parts[0], parts[1])


def attend_kernel(
    q_ref, own_ref, other_ref, query_ref, key_ref, mixed_ref, log_ref, low_bias, up_bias
):
    half = q_ref.shape[0] // 2
    low_bias[...] = bias_of(key_ref[: 2 * half], query_ref[:, :half])
    up_bias[...] = bias_of(key_ref[2 * half :], query_ref[:, half:])

    def one_pair(lanes, first, heads):
        q = q_ref[:, lanes] * jnp.asarray(HEAD_DIM**-0.5, jnp.bfloat16)
        k_low = jnp.concatenate([own_ref[0, :half, lanes], other_ref[0, :half, lanes]], axis=0)
        k_up = jnp.concatenate([own_ref[0, half:, lanes], other_ref[0, half:, lanes]], axis=0)
        v_low = jnp.concatenate([own_ref[1, :half, lanes], other_ref[1, :half, lanes]], axis=0).T
        v_up = jnp.concatenate([own_ref[1, half:, lanes], other_ref[1, half:, lanes]], axis=0).T
        low_parts, up_parts = [], []
        for number in range(heads):
            rows = slice(number * HEAD_DIM, (number + 1) * HEAD_DIM)
            q_head = only_head(q, number, heads)
            s = tail_dot(k_low, q_head[:half]) + low_bias[...]
            top = jnp.max(s, axis=0, keepdims=True)
            e = jnp.exp(s - top)
            total = jnp.sum(e, axis=0, keepdims=True)
            mixed = dot_rows(v_low[rows], e.astype(jnp.bfloat16)) / total
            low_parts.append(mixed)
            log_ref[pl.ds(first + number, 1), :half] = top + jnp.log(total)
            s_low = tail_dot(k_low, q_head[half:])
            s_up = tail_dot(k_up, q_head[half:]) + up_bias[...]
            top = jnp.maximum(
                jnp.max(s_low, axis=0, keepdims=True), jnp.max(s_up, axis=0, keepdims=True)
            )
            e_low = jnp.exp(s_low - top)
            e_up = jnp.exp(s_up - top)
            total = jnp.sum(e_low, axis=0, keepdims=True) + jnp.sum(e_up, axis=0, keepdims=True)
            mixed = dot_rows(v_low[rows], e_low.astype(jnp.bfloat16))
            mixed = mixed + dot_rows(v_up[rows], e_up.astype(jnp.bfloat16))
            up_parts.append(mixed / total)
            log_ref[pl.ds(first + number, 1), half:] = top + jnp.log(total)
        mixed_ref[:half, lanes] = jnp.concatenate(low_parts, axis=0).T.astype(jnp.bfloat16)
        mixed_ref[half:, lanes] = jnp.concatenate(up_parts, axis=0).T.astype(jnp.bfloat16)

    per_pair(one_pair)


def attend_back_kernel(
    q_ref,
    own_ref,
    other_ref,
    query_ref,
    key_ref,
    mixed_ref,
    log_ref,
    grad_ref,
    dq_ref,
    own_out,
    other_out,
    low_bias,
    up_bias,
):
    half = q_ref.shape[0] // 2
    factor = HEAD_DIM**-0.5
    low_bias[...] = bias_of(key_ref[: 2 * half], query_ref[:, :half])
    up_bias[...] = bias_of(key_ref[2 * half :], query_ref[:, half:])

    def one_pair(lanes, first, heads):
        q = q_ref[:, lanes] * jnp.asarray(factor, jnp.bfloat16)
        grad = grad_ref[:, lanes]
        product = (grad.astype(jnp.float32) * mixed_ref[:, lanes].astype(jnp.float32)).T
        q_heads = [only_head(q, number, heads) for number in range(heads)]
        grad_heads = [only_head(grad, number, heads) for number in range(heads)]
        deltas = [
            jnp.sum(product[number * HEAD_DIM : (number + 1) * HEAD_DIM], axis=0, keepdims=True)
            for number in range(heads)
        ]
        logs = [log_ref[pl.ds(first + number, 1), :] for number in range(heads)]
        dq_low = [None] * heads
        dq_up = [None] * heads
        for source, out, place in ((own_ref, own_out, 0), (other_ref, other_out, 1)):
            bias_rows = slice(place * half, (place + 1) * half)
            for upper in (False, True):
                rows = slice(half, None) if upper else slice(0, half)
                k = source[0, rows, lanes]
                v = source[1, rows, lanes]
                k_turned = k.T
                dk_parts, dv_parts = [], []
                for number in range(heads):
                    head_rows = slice(number * HEAD_DIM, (number + 1) * HEAD_DIM)
                    first_query = half if upper else 0
                    q_head = q_heads[number][first_query:]
                    grad_head = grad_heads[number][first_query:]
                    s = tail_dot(k, q_head)
                    if upper:
                        s = s + up_bias[bias_rows]
                    else:
                        s = jnp.concatenate([s[:, :half] + low_bias[bias_rows], s[:, half:]], axis=1)
                    p = jnp.exp(s - logs[number][:, first_query:])
                    dp = tail_dot(v, grad_head)
                    ds = (p * (dp - deltas[number][:, first_query:])).astype(jnp.bfloat16)
                    dv_parts.append(dot_rows(p.astype(jnp.bfloat16), grad[first_query:]))
                    dk_parts.append(dot_rows(ds, q[first_query:]))
                    turned = dot_rows(k_turned[head_rows], ds)
                    low = None if upper else turned[:, :half]
                    up = turned if upper else turned[:, half:]
                    if low is not None:
                        dq_low[number] = low if dq_low[number] is None else dq_low[number] + low
                    dq_up[number] = up if dq_up[number] is None else dq_up[number] + up
                out[0, rows, lanes] = join_heads(dk_parts).astype(jnp.bfloat16)
                out[1, rows, lanes] = join_heads(dv_parts).astype(jnp.bfloat16)
        dq_ref[:half, lanes] = (jnp.concatenate(dq_low, axis=0).T * factor).astype(jnp.bfloat16)
        dq_ref[half:, lanes] = (jnp.concatenate(dq_up, axis=0).T * factor).astype(jnp.bfloat16)

    per_pair(one_pair)


def kernel_call(body, outs, half, cost):
    return pl.pallas_call(
        body,
        out_shape=outs,
        scratch_shapes=[pltpu.VMEM((2 * half, half), jnp.float32)] * 2,
        compiler_params=pltpu.CompilerParams(vmem_limit_bytes=48 * 1024 * 1024),
        cost_estimate=pl.CostEstimate(flops=cost, bytes_accessed=12 << 20, transcendentals=cost // 256),
    )


def attend(query, own, other, query_places, key_places):
    rows, width = query.shape
    outs = (
        jax.ShapeDtypeStruct((rows, width), jnp.bfloat16),
        jax.ShapeDtypeStruct((HEADS, rows), jnp.float32),
    )
    call = kernel_call(attend_kernel, outs, rows // 2, 8 << 30)
    return call(query, own, other, query_places, key_places)


def attend_back(query, own, other, query_places, key_places, mixed, logs, grad):
    rows, width = query.shape
    outs = (
        jax.ShapeDtypeStruct((rows, width), jnp.bfloat16),
        jax.ShapeDtypeStruct(own.shape, jnp.bfloat16),
        jax.ShapeDtypeStruct(own.shape, jnp.bfloat16),
    )
    call = kernel_call(attend_back_kernel, outs, rows // 2, 24 << 30)
    return call(query, own, other, query_places, key_places, mixed, logs, grad)


ALL = ("dp", "y", "core")


def round_low(values):
    return values.astype(jnp.bfloat16)


def one_hot_columns(targets, width):
    line = lax.broadcasted_iota(jnp.int32, (width, targets.shape[0]), 0)
    return (line == targets[None, :]).astype(jnp.bfloat16)


def swap_with(values, axis, bit):
    count = lax.axis_size(axis)
    return lax.ppermute(values, axis, [(here, here ^ (1 << bit)) for here in range(count)])


def near_owners(order, dp_bits, each):
    owner = (lax.axis_index("dp") * 2 + lax.axis_index("y")) * 2 + lax.axis_index("core")
    bits = dp_bits + 2
    column = jnp.arange(each << bits, dtype=jnp.int32)
    place, inner = column // each, column % each
    far = jnp.zeros_like(place)
    for number, (axis, bit) in enumerate(order):
        weight = {"core": 0, "y": 1, "dp": 2 + bit}[axis]
        far = far + (((place >> (bits - 1 - number)) & 1) << weight)
    return (owner ^ far) * each + inner


def halve_first(left, right, order):
    half = left.shape[1] // 2
    give = round_low(lead_dot(left[:, half:], right))
    got = swap_with(give, *order[0])
    return round_low(lead_dot(left[:, :half], right) + got.astype(jnp.float32))


def halve(values, axis, bit):
    half = values.shape[0] // 2
    got = swap_with(values[half:], axis, bit)
    return round_low(values[:half].astype(jnp.float32) + got.astype(jnp.float32))


def local(tokens, positions, w_qkv, w_out, w_up, w_down, small_params, cotangent):
    seqs_here, local_len, model_width = tokens.shape
    span = local_len // 2
    rows = seqs_here * local_len
    half = rows // 2
    y = lax.axis_index("y")
    core = lax.axis_index("core")
    groups = lax.axis_size("dp")
    owners = groups * 4
    small_len = small_params.shape[0]
    whole_rows = model_width % owners == 0
    each = model_width // owners
    dp_bits = groups.bit_length() - 1

    def trade(values):
        mine = lax.dynamic_index_in_dim(values, y, 0, keepdims=False)
        give = lax.dynamic_index_in_dim(values, 1 - y, 0, keepdims=False)
        got = lax.ppermute(give, "y", SWAP)
        return jnp.concatenate([mine[:span], got[:span], mine[span:], got[span:]], axis=0)

    def trade_back(values):
        mine = jnp.concatenate([values[:span], values[half : half + span]], axis=0)
        give = jnp.concatenate([values[span:half], values[half + span :]], axis=0)
        got = lax.ppermute(give, "y", SWAP)
        first = jnp.where(y == 0, mine, got)
        second = jnp.where(y == 0, got, mine)
        return jnp.stack([first, second])

    inputs = trade(tokens)
    if whole_rows:
        blocks = jnp.concatenate(
            [w_qkv.reshape(each, 3 * model_width), w_out.reshape(each, model_width)], axis=1
        )
        room = -(each + 1) % 8
        held = each + 1 + room
        extra = jnp.pad(small_params.reshape(1, -1), [(0, room), (0, FF - small_len)])
        extra = extra.reshape(1 + room, FF)
        blocks = jnp.concatenate([blocks, extra], axis=0)
        up_block = jnp.pad(w_up.reshape(each, FF), [(0, held - each), (0, 0)])
        blocks = lax.all_gather(blocks, ALL, axis=0, tiled=True)
        up_mat = lax.all_gather(up_block, ALL, axis=0, tiled=True)
        down_mat = lax.all_gather(w_down.reshape(-1, model_width), ALL, axis=0, tiled=True)
        qkv_mat = blocks[:, : 3 * model_width]
        out_mat = blocks[:, 3 * model_width :]
        packed = blocks.reshape(owners, held, FF)[:, each, :small_len].reshape(-1)
        column = jnp.arange(owners * held, dtype=jnp.int32)
        inside = column % held
        spread = jnp.where(inside < each, column // held * each + inside, -1)
        spread = one_hot_columns(spread, model_width)

        def widen(values):
            return round_low(dot_rows(values, spread))

        def narrow(values):
            return tail_dot(round_low(values), spread)

    else:
        small_width = -(-small_len // LANES)
        qkv_width = w_qkv.shape[0] // LANES
        blocks = jnp.concatenate(
            [w_qkv.reshape(LANES, qkv_width), pack_small(small_params, small_width)], axis=1
        )
        blocks = gather_packed(blocks, core)
        qkv_mat = blocks[..., :qkv_width].reshape(model_width, 3 * model_width)
        packed = blocks[..., qkv_width:].reshape(owners, -1)[:, :small_len].reshape(-1)
        out_mat = gather_packed(w_out.reshape(LANES, -1), core).reshape(model_width, model_width)
        up_mat = gather_packed(w_up.reshape(LANES, -1), core).reshape(model_width, FF)
        down_mat = gather_packed(w_down.reshape(LANES, -1), core).reshape(FF, model_width)

        def widen(values):
            return values

        def narrow(values):
            return values

    grad_rows = trade(cotangent)
    packed = packed.astype(jnp.float32)
    pieces = [packed[number * model_width : (number + 1) * model_width] for number in range(7)]
    gain_one, bias_one, bias_query, bias_value, bias_out, gain_two, bias_two = pieces
    up_bias = packed[7 * model_width : 7 * model_width + FF]
    down_bias = packed[7 * model_width + FF :]

    place_row = lax.dynamic_index_in_dim(positions, y, 0, keepdims=False)

    def places_of(core_index):
        near = lax.dynamic_slice_in_dim(place_row, (2 * y + core_index) * local_len, local_len)
        far = lax.dynamic_slice_in_dim(place_row, (2 - 2 * y + core_index) * local_len, local_len)
        return jnp.concatenate([near[:span], far[:span]]), jnp.concatenate([near[span:], far[span:]])

    own_low, own_up = places_of(core)
    other_low, other_up = places_of(1 - core)
    query_places = jnp.concatenate([own_low, own_up])[None, :]
    key_places = jnp.concatenate([own_low, other_low, own_up, other_up])[:, None]

    inputs = inputs.astype(jnp.float32)
    normed_one, inverse_one = layer_stats(inputs)
    act_one = round_low(normed_one * gain_one + bias_one)
    qkv_bias = jnp.concatenate([bias_query, jnp.zeros_like(bias_query), bias_value])
    qkv_rows = round_low(dot_rows(widen(act_one), qkv_mat) + qkv_bias)
    query = qkv_rows[:, :model_width]
    own_kv = jnp.stack([qkv_rows[:, model_width : 2 * model_width], qkv_rows[:, 2 * model_width :]])
    other_kv = lax.ppermute(own_kv, "core", SWAP)
    mixed, logs = attend(query, own_kv, other_kv, query_places, key_places)
    resid = inputs + dot_rows(widen(mixed), out_mat) + bias_out
    normed_two, inverse_two = layer_stats(resid)
    act_two = round_low(normed_two * gain_two + bias_two)
    pre_act = dot_rows(widen(act_two), up_mat) + up_bias
    gelu_rows = round_low(smooth_gate(pre_act))
    outputs = resid + dot_rows(gelu_rows, down_mat) + down_bias
    result = trade_back(round_low(outputs))

    if whole_rows:
        steps = [("dp", bit) for bit in range(dp_bits)]
        order_a = [("core", 0), steps[0], ("y", 0)] + steps[1:]
        order_b = [("core", 0), ("y", 0), steps[0]] + steps[1:]
        turn_a = one_hot_columns(near_owners(order_a, dp_bits, each), model_width)
        turn_b = one_hot_columns(near_owners(order_b, dp_bits, each), model_width)

        def send_sum(left, right, extra=None):
            cut = (right.shape[1] // 256) * 128
            left_a = round_low(dot_rows(left, turn_a))
            left_b = round_low(dot_rows(left, turn_b))
            part_a = halve_first(left_a, right[:, :cut], order_a)
            part_b = halve_first(left_b, right[:, cut:], order_b)
            if extra is not None:
                extra = extra.reshape(model_width, -1)
                extra = round_low(lead_dot(turn_b, extra))
                part_b = jnp.concatenate([part_b, halve(extra, *order_b[0])], axis=1)
            for step_a, step_b in zip(order_a[1:3], order_b[1:3]):
                part_a, part_b = halve(part_a, *step_a), halve(part_b, *step_b)
            part = jnp.concatenate([part_a, part_b], axis=1)
            for step in order_a[3:]:
                part = halve(part, *step)
            return part

    else:

        def send_sum(left, right, extra=None):
            grad = round_low(lead_dot(left, right)).reshape(groups * 2, 2, LANES, -1)
            if extra is not None:
                extra = extra.reshape(groups * 2, 2, small_len)
                grad = jnp.concatenate([grad, pack_small(extra, small_width)], axis=-1)
            return scatter_packed(grad, core)

    grad_float = grad_rows.astype(jnp.float32)
    sum_down = round_low(lead_dot(gelu_rows, grad_rows)).reshape(owners, -1, model_width)
    sum_down = lax.psum_scatter(sum_down, ALL, scatter_dimension=0, tiled=True)
    down_bias_term = jnp.sum(grad_float, axis=0)
    grad_gelu = tail_dot(grad_rows, down_mat)
    gelu_pull = jax.vjp(smooth_gate, pre_act)[1]
    grad_pre = round_low(gelu_pull(grad_gelu)[0])
    sum_up = send_sum(act_two, grad_pre)
    up_bias_term = jnp.sum(grad_pre.astype(jnp.float32), axis=0)
    grad_act_two = narrow(tail_dot(grad_pre, up_mat))
    gain_two_term = jnp.sum(grad_act_two * normed_two, axis=0)
    bias_two_term = jnp.sum(grad_act_two, axis=0)
    grad_resid = grad_float + norm_back(grad_act_two, normed_two, inverse_two, gain_two)
    grad_attn = round_low(grad_resid)
    sum_out = send_sum(mixed, grad_attn)
    bias_out_term = jnp.sum(grad_attn.astype(jnp.float32), axis=0)
    grad_mixed = round_low(narrow(tail_dot(grad_attn, out_mat)))
    grad_query, grad_own, grad_other = attend_back(
        query, own_kv, other_kv, query_places, key_places, mixed, logs, grad_mixed
    )
    grad_got = lax.ppermute(grad_other, "core", SWAP)
    grad_kv = round_low(grad_own.astype(jnp.float32) + grad_got.astype(jnp.float32))
    grad_qkv_rows = jnp.concatenate([grad_query, grad_kv[0], grad_kv[1]], axis=1)
    qkv_sums = jnp.sum(grad_qkv_rows.astype(jnp.float32), axis=0)
    grad_act_one = narrow(tail_dot(grad_qkv_rows, qkv_mat))
    gain_one_term = jnp.sum(grad_act_one * normed_one, axis=0)
    bias_one_term = jnp.sum(grad_act_one, axis=0)
    small_grad = jnp.concatenate(
        [
            gain_one_term,
            bias_one_term,
            qkv_sums[:model_width],
            qkv_sums[2 * model_width :],
            bias_out_term,
            gain_two_term,
            bias_two_term,
            up_bias_term,
            down_bias_term,
        ]
    )
    sum_qkv = send_sum(act_one, grad_qkv_rows, round_low(small_grad))
    grad_input = grad_resid + norm_back(grad_act_one, normed_one, inverse_one, gain_one)
    grad_tokens = trade_back(round_low(grad_input))
    main = w_qkv.shape[0] // sum_qkv.shape[0]
    grad_qkv = sum_qkv[:, :main].astype(jnp.float32).reshape(-1)
    grad_small = sum_qkv[:, main:].astype(jnp.float32).reshape(-1)[:small_len]
    grad_out, grad_up, grad_down = [
        piece.astype(jnp.float32).reshape(-1) for piece in (sum_out, sum_up, sum_down)
    ]
    return (result, grad_tokens, grad_qkv, grad_out, grad_up, grad_down, grad_small)


def solution(mesh):
    groups, owners = mesh.shape["dp"], mesh.shape["ctx"]
    fine = Mesh(mesh.devices.reshape(groups, owners // 2, 2), ("dp", "y", "core"))
    rows = P("dp", ("y", "core"), None)
    flat = P(("dp", "y", "core"))
    return jax.shard_map(
        local,
        mesh=fine,
        in_specs=(rows, P("dp", None), flat, flat, flat, flat, flat, rows),
        out_specs=(rows, rows, flat, flat, flat, flat, flat),
        check_vma=False,
    )
```

time: 1150 us -> 642 us (0.56)
  waiting for transfers between devices: 537 us -> 268 us
  local copies, waits for them, and re-layouts: 226 us -> 85 us
  other arithmetic: 154 us -> 35.2 us
  Pallas kernels: 0 us -> 43.8 us
  matrix products: 199 us -> 156 us
  starting transfers between devices: 7.24 us -> 28.5 us
    unnamed x12 -> x5, waiting for transfers between devices: 251 us -> 0.07 us
    reshape x15 -> x10, local copies, waits for them, and re-layouts: 124 us -> 10.8 us  [the longest x3 3.77 us: local(): piece.astype(jnp.float32).reshape(-1)]
    dot_general x10, matrix products: 132 us -> 65.2 us  [dot_rows(): lax.dot_general(left, right, (((1,), (0,)), ((), ())), preferred_element_...]
    all_gather x4 -> x3, waiting for transfers between devices: 204 us -> 149 us  [the longest x1 70.6 us: local(): blocks = lax.all_gather(blocks, ALL, axis=0, tiled=True)]
    convert_element_type x7 -> x21, other arithmetic: 57.9 us -> 12.3 us  [the longest x20 11.1 us: round_low(): return values.astype(jnp.bfloat16)]
    pallas_call x0 -> x2, Pallas kernels: none -> 43.8 us  [the longest x1 25.8 us: attend_back(): return call(query, own, other, query_places, key_places, mixed, logs, grad)]
    ppermute x14 -> x31, waiting for transfers between devices: 81.9 us -> 120 us  [the longest x25 107 us: swap_with(): lax.ppermute(values, axis, [(here, here ^ 1 << bit) for here in range(cou...]
    all_gather x4 -> x0, local copies, waits for them, and re-layouts: 23.3 us -> none  [gather_packed(): own = lax.all_gather(block, OWNERS, axis=0, tiled=True)]
  transfers between devices with their start and end apart: 22 -> 35, of which waited for: 11 -> 18; matrix products, arithmetic and copies ran while one was open for 30% -> 39% of each run, Pallas kernels for 0% -> 7%
where the time goes in v2:
time: 642 us; the launch traced here: 633 us
  waiting for transfers between devices  268 us (42%)
  matrix products  156 us (24%)
  local copies, waits for them, and re-layouts  85 us (13%)
  Pallas kernels  43.8 us (7%)
  other arithmetic  35.2 us (5%)
  starting transfers between devices  28.5 us (4%)
  between operations  15.3 us (2%)
    ppermute x25, waiting for transfers between devices, swap_with(): lax.ppermute(values, axis, [(here, here ^ 1 << bit) for here in range(cou...  107 us
    all_gather x1, waiting for transfers between devices, local(): blocks = lax.all_gather(blocks, ALL, axis=0, tiled=True)  70.6 us
    all_gather x1, waiting for transfers between devices, local(): lax.all_gather(w_down.reshape(-1, model_width), ALL, axis=0, tiled=True)  69.6 us
    dot_general x10, matrix products, dot_rows(): lax.dot_general(left, right, (((1,), (0,)), ((), ())), preferred_element_...  65.2 us
    dot_general x4, matrix products, tail_dot(): lax.dot_general(left_side, right_side, (((1,), (1,)), ((), ())), preferre...  53.7 us
    dot_general x14, matrix products, lead_dot(): lax.dot_general(left_side, right_side, (((0,), (0,)), ((), ())), preferre...  37.4 us
    pallas_call x1, Pallas kernels, attend_back(): return call(query, own, other, query_places, key_places, mixed, logs, grad)  25.8 us
    ppermute x25, starting transfers between devices, swap_with(): lax.ppermute(values, axis, [(here, here ^ 1 << bit) for here in range(cou...  22.8 us
  transfers between devices with their start and end apart: 35, of which 18 were waited for; matrix products, arithmetic and copies ran while one was open for 39% of the time, Pallas kernels for 7%

profile of v2, /device:TPU:0, one launch (start us, length us, event | category | flops | bytes accessed | tf_op | source)
XLA Modules:
  0.0 632.7 jit_solution(16631658159344089269)
XLA Ops:
  21.9 12.5 %collective-permute-done = bf16[256,1088]{0,1:T(8,128)(2,1)S(1)} collective-permute-done((bf16[256,1088]{0,1:T(8,128)(2,1)}, bf16[256,1088]{0,1:T(8,128)(2,1)S(1)}, u32[]{:S(2)}, u32[]{:S(2)}) %collective-permute-start) | collective-permute-done | bytes 557088 | tf_op jit(solution)/shard_map/ppermute | solution.py:311
  35.1 70.6 %all-gather.4.cloned.1.call-done = bf16[1280,4352]{1,0:T(8,128)(2,1)} async-done(((bf16[40,4352]{1,0:T(8,128)(2,1)}), bf16[1280,4352]{1,0:T(8,128)(2,1)}) %all-gather.4.cloned.1.call-update) | async-done | bytes 11141136 | tf_op jit(solution)/shard_map/all_gather | solution.py:333
  107.8 12.1 %add_convert_fusion = bf16[512,3264]{1,0:T(8,128)(2,1)} fusion(bf16[1280,4352]{1,0:T(8,128)(2,1)} %all-gather.4.cloned.1.call-done, f32[3264]{0:T(1024)S(1)} %concatenate.65, s32[1280]{0:T(1024)S(1)} %fusion.134, f32[1088]{0:T(1024)S(1)} %get-tuple-element.71, f32[1088]{0:T(1024)S(1)} %get-tuple-element.72, f32[512]{0:T(512)S(1)} %add_rsqrt_fusion.1, ...), kind=kOutput, calls=%fused_computation.15 | convolution fusion | flops 5716885504 | bytes 13007104 | tf_op jit(solution)/shard_map/dot_general | solution.py:72
  152.1 18.0 %shard_map.135 = (bf16[512,1088]{1,0:T(8,128)(2,1)S(1)}, f32[17,512]{1,0:T(8,128)S(1)}) custom-call(bf16[512,1088]{1,0:T(8,128)(2,1)S(1)} %get-tuple-element.42.q_ref, bf16[2,512,1088]{2,1,0:T(8,128)(2,1)S(1)} %pad_maximum_fusion.own_ref, bf16[2,512,1088]{2,1,0:T(8,128)(2,1)} %copy.37.other_ref, s32[1,512]{1,0:T(1,128)S(1)} %bitcast.79, s32[1024,1]{1,0:T(8,128)S(1)} %copy-done.1), custom_call_target="tpu_custom_call" | custom-call | flops 8589934592 | bytes 12582912 | tf_op jit(solution)/shard_map/pallas_call | solution.py:238
  171.8 6.4 %fusion.155 = (f32[512]{0:T(512)S(1)}, f32[512,1088]{0,1:T(8,128)S(1)}) fusion(f32[1088]{0:T(1024)} %get-tuple-element.68, bf16[1280,4352]{1,0:T(8,128)(2,1)} %all-gather.4.cloned.1.call-done, bf16[512,1088]{1,0:T(8,128)(2,1)} %copy-done.3, s32[1280]{0:T(1024)} %copy-done.46, bf16[128,1088]{0,1:T(8,128)(2,1)} %copy-done.14, ...), kind=kOutput, calls=%fused_computation.274 | convolution fusion | flops 2860301824 | bytes 7489536 | tf_op jit(solution)/shard_map/dot_general | solution.py:72
  188.8 8.5 %all-gather.6.cloned.1.call-done = bf16[1280,4352]{1,0:T(8,128)(2,1)} async-done(((bf16[40,4352]{1,0:T(8,128)(2,1)}), bf16[1280,4352]{1,0:T(8,128)(2,1)}) %all-gather.6.cloned.1.call-update) | async-done | bytes 11141136 | tf_op jit(solution)/shard_map/all_gather | solution.py:334
  197.3 16.3 %fusion.159 = f32[512,4352]{1,0:T(8,128)} fusion(bf16[1280,4352]{1,0:T(8,128)(2,1)} %all-gather.6.cloned.1.call-done, bf16[512,1088]{0,1:T(8,128)(2,1)} %copy-done.20, s32[1280]{0:T(1024)S(1)} %copy-done.47), kind=kOutput, calls=%fused_computation.276 | convolution fusion | flops 7132364800 | bytes 21173248 | tf_op jit(solution)/shard_map/dot_general | solution.py:72
  213.6 69.6 %all-gather.8.cloned.1.call-done = bf16[4352,1088]{1,0:T(8,128)(2,1)} async-done(((bf16[136,1088]{1,0:T(8,128)(2,1)}), bf16[4352,1088]{1,0:T(8,128)(2,1)}) %all-gather.8.cloned.1.call-update) | async-done | bytes 9469968 | tf_op jit(solution)/shard_map/all_gather | solution.py:335
  283.2 13.0 %fusion.38 = bf16[512,1088]{0,1:T(8,128)(2,1)} fusion(f32[512,1088]{0,1:T(8,128)S(1)} %get-tuple-element.76, bf16[4352,1088]{1,0:T(8,128)(2,1)} %all-gather.8.cloned.1.call-done, f32[1088]{0:T(1024)S(1)} %copy-done.43, f32[512,4352]{1,0:T(8,128)} %fusion.159, f32[4352]{0:T(1024)S(1)} %copy-done.37), kind=kOutput, calls=%fused_computation.59 | convolution fusion | flops 4872568832 | bytes 21746944 | tf_op jit(solution)/shard_map/dot_general | solution.py:72
  300.8 11.1 %convolution_convert_fusion = bf16[4352,1088]{0,1:T(8,128)(2,1)} fusion(bf16[128,1088]{0,1:T(8,128)(2,1)S(1)} %copy-done.24, bf16[128,1088]{0,1:T(8,128)(2,1)S(1)} %copy-done.23, bf16[128,1088]{0,1:T(8,128)(2,1)S(1)} %copy-done.25, bf16[128,1088]{0,1:T(8,128)(2,1)S(1)} %copy-done.22, f32[512,4352]{1,0:T(8,128)} %fusion.159, f32[4352]{0:T(1024)S(1)} %copy-done.37), kind=kOutput, calls=%fused_computation | convolution fusion | flops 4880089088 | bytes 19514368 | tf_op jit(solution)/shard_map/dot_general | solution.py:32
  311.9 16.8 %fusion.158 = (bf16[4352]{0:T(1024)(128)(2,1)}, bf16[512,4352]{1,0:T(8,128)(2,1)}) fusion(f32[512,4352]{1,0:T(8,128)} %fusion.159, f32[4352]{0:T(1024)S(1)} %copy-done.37, bf16[4352,1088]{1,0:T(8,128)(2,1)S(1)} %bitcast.85, bf16[128,1088]{0,1:T(8,128)(2,1)S(1)} %copy-done.24, bf16[128,1088]{0,1:T(8,128)(2,1)S(1)} %copy-done.23, ...), kind=kOutput, calls=%fused_computation.275 | convolution fusion | flops 4902088704 | bytes 23979520 | tf_op jit(solution)/shard_map/dot_general | solution.py:38
  328.7 16.8 %multiply_reduce_fusion = (bf16[1088]{0:T(1024)(128)(2,1)}, f32[512]{0:T(512)S(1)}, f32[512]{0:T(512)S(1)}, bf16[1088]{0:T(1024)(128)(2,1)}, f32[512,1088]{0,1:T(8,128)}) fusion(f32[512,1088]{0,1:T(8,128)S(1)} %get-tuple-element.76, f32[512]{0:T(512)S(1)} %add_rsqrt_fusion, f32[512]{0:T(512)S(1)} %broadcast_multiply_fusion.4, ...), kind=kOutput, calls=%fused_computation.95 | convolution fusion | flops 7137375232 | bytes 20076032 | tf_op jit(solution)/shard_map/dot_general | solution.py:38
  349.9 6.2 fusion.37
  359.9 25.8 %shard_map.136 = (bf16[512,1088]{1,0:T(8,128)(2,1)S(1)}, bf16[2,512,1088]{2,1,0:T(8,128)(2,1)}, bf16[2,512,1088]{2,1,0:T(8,128)(2,1)}) custom-call(bf16[512,1088]{1,0:T(8,128)(2,1)S(1)} %get-tuple-element.42.q_ref, bf16[2,512,1088]{2,1,0:T(8,128)(2,1)} %copy-done, bf16[2,512,1088]{2,1,0:T(8,128)(2,1)} %copy.37.other_ref, s32[1,512]{1,0:T(1,128)S(1)} %bitcast.80, ...), custom_call_target="tpu_custom_call" | custom-call | flops 25769803776 | bytes 12582912 | tf_op jit(solution)/shard_map/pallas_call | solution.py:249
  393.1 4.7 convolution_convert_fusion.1
  407.0 13.9 %copy.45 = bf16[4352,1088]{1,0:T(8,128)(2,1)} copy(bf16[4352,1088]{0,1:T(8,128)(2,1)} %convolution_convert_fusion) | data formatting | bytes 18939904 | tf_op jit(solution)/shard_map/convert_element_type | solution.py:256
  457.7 13.9 %fusion.73 = (bf16[1088]{0:T(1024)(128)(2,1)}, f32[512]{0:T(512)}, f32[512]{0:T(512)}, bf16[1088]{0:T(1024)(128)(2,1)}, f32[512,1088]{0,1:T(8,128)}) fusion(f32[512]{0:T(512)} %copy-done.41, f32[512]{0:T(512)S(1)} %copy-done.39, bf16[128,1088]{0,1:T(8,128)(2,1)} %copy-done.14, bf16[128,1088]{0,1:T(8,128)(2,1)} %copy-done.10, ...), kind=kOutput, calls=%fused_computation.93 | convolution fusion | flops 5715768320 | bytes 15294976 | tf_op jit(solution)/shard_map/dot_general | solution.py:38
  484.4 5.5 concatenate.76
  511.0 29.1 %collective-permute-done.27 = bf16[272,2176]{1,0:T(8,128)(2,1)S(1)} collective-permute-done((bf16[272,2176]{1,0:T(8,128)(2,1)S(1)}, bf16[272,2176]{1,0:T(8,128)(2,1)S(1)}, u32[]{:S(2)}, u32[]{:S(2)}) %collective-permute-start.27) | collective-permute-done | bytes 1183776 | tf_op jit(solution)/shard_map/ppermute | solution.py:266
  547.7 11.3 %collective-permute-done.28 = bf16[136,2176]{1,0:T(8,128)(2,1)S(1)} collective-permute-done((bf16[136,2176]{1,0:T(8,128)(2,1)S(1)}, bf16[136,2176]{1,0:T(8,128)(2,1)S(1)}, u32[]{:S(2)}, u32[]{:S(2)}) %collective-permute-start.28) | collective-permute-done | bytes 591904 | tf_op jit(solution)/shard_map/ppermute | solution.py:266
  562.7 12.9 %collective-permute-done.7 = bf16[272,1536]{1,0:T(8,128)(2,1)S(1)} collective-permute-done((bf16[272,1536]{1,0:T(8,128)(2,1)S(1)}, bf16[272,1536]{1,0:T(8,128)(2,1)S(1)}, u32[]{:S(2)}, u32[]{:S(2)}) %collective-permute-start.7) | collective-permute-done | bytes 835616 | tf_op jit(solution)/shard_map/ppermute | solution.py:266
  582.7 6.1 collective-permute-done.8
  594.9 13.6 %collective-permute-done.13 = bf16[68,3276]{1,0:T(8,128)(2,1)S(1)} collective-permute-done((bf16[68,3276]{1,0:T(8,128)(2,1)S(1)}, bf16[68,3276]{1,0:T(8,128)(2,1)S(1)}, u32[]{:S(2)}, u32[]{:S(2)}) %collective-permute-start.13) | collective-permute-done | bytes 445568 | tf_op jit(solution)/shard_map/ppermute | solution.py:266
  610.5 11.2 %collective-permute-done.14 = bf16[34,3276]{1,0:T(8,128)(2,1)S(1)} collective-permute-done((bf16[34,3276]{1,0:T(8,128)(2,1)S(1)}, bf16[34,3276]{1,0:T(8,128)(2,1)S(1)}, u32[]{:S(2)}, u32[]{:S(2)}) %collective-permute-start.14) | collective-permute-done | bytes 222800 | tf_op jit(solution)/shard_map/ppermute | solution.py:266
  (334 shorter events, 191.5 us)
Async XLA Ops:
  7.2 98.5 %all-gather.4.cloned.1.call-start = ((), (), s32[]{:S(2)}) async-start(), calls=%async_computation.1 | async-start | bytes 11489280 | tf_op jit(solution)/shard_map/all_gather | solution.py:333
  11.1 186.2 %all-gather.6.cloned.1.call-start = ((), (), s32[]{:S(2)}) async-start(), calls=%async_computation.2 | async-start | bytes 11489280 | tf_op jit(solution)/shard_map/all_gather | solution.py:334
  13.3 269.9 %all-gather.8.cloned.1.call-start = ((), (), s32[]{:S(2)}) async-start(), calls=%async_computation.3 | async-start | bytes 10340352 | tf_op jit(solution)/shard_map/all_gather | solution.py:335
  14.4 609.2 %reduce-scatter.4.cloned.1.call-start = ((), (), s32[]{:S(2)}) async-start(), calls=%async_computation.4 | async-start | bytes 10340352
  15.3 19.1 %collective-permute-start = (bf16[256,1088]{0,1:T(8,128)(2,1)}, bf16[256,1088]{0,1:T(8,128)(2,1)S(1)}, u32[]{:S(2)}, u32[]{:S(2)}) collective-permute-start(bf16[256,1088]{0,1:T(8,128)(2,1)} %dynamic-slice_bitcast_fusion.1), channel_id=1, source_target_pairs={{0,2},{2,0},{1,3},{3,1},{4,6},{6,4},{5,7},{7,5},{8,10},{10,8},{9,1... | collective-permute-start | bytes 1671176 | tf_op jit(solution)/shard_map/ppermute | solution.py:311
  19.1 116.7 %collective-permute-start.3 = (bf16[256,1088]{0,1:T(8,128)(2,1)}, bf16[256,1088]{0,1:T(8,128)(2,1)}, u32[]{:S(2)}, u32[]{:S(2)}) collective-permute-start(bf16[256,1088]{0,1:T(8,128)(2,1)} %dynamic-slice_bitcast_fusion), channel_id=1, source_target_pairs={{0,2},{2,0},{1,3},{3,1},{4,6},{6,4},{5,7},{7,5},{8,10},{10,8},{9,1... | collective-permute-start | bytes 1671176 | tf_op jit(solution)/shard_map/ppermute | solution.py:311
  126.0 21.0 %collective-permute-start.1 = (bf16[2,512,1088]{1,2,0:T(8,128)(2,1)}, bf16[2,512,1088]{1,2,0:T(8,128)(2,1)}, u32[]{:S(2)}, u32[]{:S(2)}) collective-permute-start(bf16[2,512,1088]{1,2,0:T(8,128)(2,1)} %copy.36), channel_id=1, source_target_pairs={{0,1},{1,0},{2,3},{3,2},{4,5},{5,4},{6,7},{7,6},{8,9},{9,8},{10,11... | collective-permute-start | bytes 6684680 | tf_op jit(solution)/shard_map/ppermute | solution.py:395
  299.3 136.0 %collective-permute-start.2 = (bf16[256,1088]{0,1:T(8,128)(2,1)}, bf16[256,1088]{0,1:T(8,128)(2,1)}, u32[]{:S(2)}, u32[]{:S(2)}) collective-permute-start(bf16[256,1088]{0,1:T(8,128)(2,1)} %pad_maximum_fusion.18), channel_id=1, source_target_pairs={{0,2},{2,0},{1,3},{3,1},{4,6},{6,4},{5,7},{7,5},{8,10},{10,8},{9,1... | collective-permute-start | bytes 1671176 | tf_op jit(solution)/shard_map/ppermute | solution.py:317
  390.1 55.5 %collective-permute-start.4 = (bf16[2,512,1088]{1,2,0:T(8,128)(2,1)}, bf16[2,512,1088]{1,2,0:T(8,128)(2,1)}, u32[]{:S(2)}, u32[]{:S(2)}) collective-permute-start(bf16[2,512,1088]{1,2,0:T(8,128)(2,1)} %copy.42), channel_id=1, source_target_pairs={{0,1},{1,0},{2,3},{3,2},{4,5},{5,4},{6,7},{7,6},{8,9},{9,8},{10,11... | collective-permute-start | bytes 6684680 | tf_op jit(solution)/shard_map/ppermute | solution.py:458
  397.8 101.6 %collective-permute-start.26 = (bf16[544,2176]{1,0:T(8,128)(2,1)}, bf16[544,2176]{1,0:T(8,128)(2,1)}, u32[]{:S(2)}, u32[]{:S(2)}) collective-permute-start(bf16[544,2176]{1,0:T(8,128)(2,1)} %convolution_convert_fusion.1), channel_id=1, source_target_pairs={{0,1},{1,0},{2,3},{3,2},{4,5},{5,4},{6,7},{7,6},{8,9},{9,8},{10,11... | collective-permute-start | bytes 7102472 | tf_op jit(solution)/shard_map/ppermute | solution.py:266
  401.4 19.6 %collective-permute-start.16 = (bf16[272,512]{1,0:T(8,128)(2,1)}, bf16[272,512]{1,0:T(8,128)(2,1)}, u32[]{:S(2)}, u32[]{:S(2)}) collective-permute-start(bf16[272,512]{1,0:T(8,128)(2,1)} %slice.510), channel_id=1, source_target_pairs={{0,4},{4,0},{8,12},{12,8},{16,20},{20,16},{24,28},{28,24},{1,5},{5... | collective-permute-start | bytes 835592 | tf_op jit(solution)/shard_map/ppermute | solution.py:266
  402.8 20.3 %collective-permute-start.19 = (bf16[272,576]{1,0:T(8,128)(2,1)S(1)}, bf16[272,576]{1,0:T(8,128)(2,1)S(1)}, u32[]{:S(2)}, u32[]{:S(2)}) collective-permute-start(bf16[272,576]{1,0:T(8,128)(2,1)S(1)} %slice.517), channel_id=1, source_target_pairs={{0,2},{2,0},{1,3},{3,1},{4,6},{6,4},{5,7},{7,5},{8,10},{10,8},{9,1... | collective-permute-start | bytes 940040 | tf_op jit(solution)/shard_map/ppermute | solution.py:266
  421.0 82.9 %collective-permute-start.23 = (bf16[544,2176]{1,0:T(8,128)(2,1)}, bf16[544,2176]{1,0:T(8,128)(2,1)}, u32[]{:S(2)}, u32[]{:S(2)}) collective-permute-start(bf16[544,2176]{1,0:T(8,128)(2,1)} %convolution_convert_fusion.2), channel_id=1, source_target_pairs={{0,1},{1,0},{2,3},{3,2},{4,5},{5,4},{6,7},{7,6},{8,9},{9,8},{10,11... | collective-permute-start | bytes 7102472 | tf_op jit(solution)/shard_map/ppermute | solution.py:266
  483.0 25.6 %collective-permute-start.5 = (bf16[256,1088]{0,1:T(8,128)(2,1)}, bf16[256,1088]{0,1:T(8,128)(2,1)}, u32[]{:S(2)}, u32[]{:S(2)}) collective-permute-start(bf16[256,1088]{0,1:T(8,128)(2,1)} %pad_maximum_fusion.20), channel_id=1, source_target_pairs={{0,2},{2,0},{1,3},{3,1},{4,6},{6,4},{5,7},{7,5},{8,10},{10,8},{9,1... | collective-permute-start | bytes 1671176 | tf_op jit(solution)/shard_map/ppermute | solution.py:317
  497.4 47.9 %collective-permute-start.9 = (bf16[544,1728]{1,0:T(8,128)(2,1)S(1)}, bf16[544,1728]{1,0:T(8,128)(2,1)S(1)}, u32[]{:S(2)}, u32[]{:S(2)}) collective-permute-start(bf16[544,1728]{1,0:T(8,128)(2,1)S(1)} %convolution_convert_fusion.3), channel_id=1, source_target_pairs={{0,1},{1,0},{2,3},{3,2},{4,5},{5,4},{6,7},{7,6},{8,9},{9,8},{10,11... | collective-permute-start | bytes 5640200 | tf_op jit(solution)/shard_map/ppermute | solution.py:266
  499.1 43.8 %collective-permute-start.6 = (bf16[544,1536]{1,0:T(8,128)(2,1)S(1)}, bf16[544,1536]{1,0:T(8,128)(2,1)S(1)}, u32[]{:S(2)}, u32[]{:S(2)}) collective-permute-start(bf16[544,1536]{1,0:T(8,128)(2,1)S(1)} %convolution_convert_fusion.4), channel_id=1, source_target_pairs={{0,1},{1,0},{2,3},{3,2},{4,5},{5,4},{6,7},{7,6},{8,9},{9,8},{10,11... | collective-permute-start | bytes 5013512 | tf_op jit(solution)/shard_map/ppermute | solution.py:266
  502.7 37.3 %collective-permute-start.27 = (bf16[272,2176]{1,0:T(8,128)(2,1)S(1)}, bf16[272,2176]{1,0:T(8,128)(2,1)S(1)}, u32[]{:S(2)}, u32[]{:S(2)}) collective-permute-start(bf16[272,2176]{1,0:T(8,128)(2,1)S(1)} %slice.535), channel_id=1, source_target_pairs={{0,2},{2,0},{1,3},{3,1},{4,6},{6,4},{5,7},{7,5},{8,10},{10,8},{9,1... | collective-permute-start | bytes 3551240 | tf_op jit(solution)/shard_map/ppermute | solution.py:266
  507.4 34.3 %collective-permute-start.24 = (bf16[272,2176]{1,0:T(8,128)(2,1)S(1)}, bf16[272,2176]{1,0:T(8,128)(2,1)S(1)}, u32[]{:S(2)}, u32[]{:S(2)}) collective-permute-start(bf16[272,2176]{1,0:T(8,128)(2,1)S(1)} %slice.528), channel_id=1, source_target_pairs={{0,4},{4,0},{8,12},{12,8},{16,20},{20,16},{24,28},{28,24},{1,5},{5... | collective-permute-start | bytes 3551240 | tf_op jit(solution)/shard_map/ppermute | solution.py:266
  540.4 18.6 %collective-permute-start.28 = (bf16[136,2176]{1,0:T(8,128)(2,1)S(1)}, bf16[136,2176]{1,0:T(8,128)(2,1)S(1)}, u32[]{:S(2)}, u32[]{:S(2)}) collective-permute-start(bf16[136,2176]{1,0:T(8,128)(2,1)S(1)} %slice.537), channel_id=1, source_target_pairs={{0,4},{4,0},{8,12},{12,8},{16,20},{20,16},{24,28},{28,24},{1,5},{5... | collective-permute-start | bytes 1775624 | tf_op jit(solution)/shard_map/ppermute | solution.py:266
  542.0 18.6 %collective-permute-start.25 = (bf16[136,2176]{1,0:T(8,128)(2,1)S(1)}, bf16[136,2176]{1,0:T(8,128)(2,1)S(1)}, u32[]{:S(2)}, u32[]{:S(2)}) collective-permute-start(bf16[136,2176]{1,0:T(8,128)(2,1)S(1)} %slice.530), channel_id=1, source_target_pairs={{0,2},{2,0},{1,3},{3,1},{4,6},{6,4},{5,7},{7,5},{8,10},{10,8},{9,1... | collective-permute-start | bytes 1775624 | tf_op jit(solution)/shard_map/ppermute | solution.py:266
  544.1 31.4 %collective-permute-start.7 = (bf16[272,1536]{1,0:T(8,128)(2,1)S(1)}, bf16[272,1536]{1,0:T(8,128)(2,1)S(1)}, u32[]{:S(2)}, u32[]{:S(2)}) collective-permute-start(bf16[272,1536]{1,0:T(8,128)(2,1)S(1)} %slice.488), channel_id=1, source_target_pairs={{0,4},{4,0},{8,12},{12,8},{16,20},{20,16},{24,28},{28,24},{1,5},{5... | collective-permute-start | bytes 2506760 | tf_op jit(solution)/shard_map/ppermute | solution.py:266
  546.7 34.8 %collective-permute-start.11 = (bf16[272,1740]{1,0:T(8,128)(2,1)S(1)}, bf16[272,1740]{1,0:T(8,128)(2,1)S(1)}, u32[]{:S(2)}, u32[]{:S(2)}) collective-permute-start(bf16[272,1740]{1,0:T(8,128)(2,1)S(1)} %pad_maximum_fusion.7), channel_id=1, source_target_pairs={{0,2},{2,0},{1,3},{3,1},{4,6},{6,4},{5,7},{7,5},{8,10},{10,8},{9,1... | collective-permute-start | bytes 2839688 | tf_op jit(solution)/shard_map/ppermute | solution.py:266
  560.9 33.0 %collective-permute-start.29 = (bf16[68,4352]{1,0:T(8,128)(2,1)S(1)}, bf16[68,4352]{1,0:T(8,128)(2,1)S(1)}, u32[]{:S(2)}, u32[]{:S(2)}) collective-permute-start(bf16[68,4352]{1,0:T(8,128)(2,1)S(1)} %pad_maximum_fusion.12), channel_id=1, source_target_pairs={{0,8},{4,12},{8,0},{12,4},{16,24},{20,28},{24,16},{28,20},{1,9},{5... | collective-permute-start | bytes 1775624 | tf_op jit(solution)/shard_map/ppermute | solution.py:266
  591.9 16.6 %collective-permute-start.13 = (bf16[68,3276]{1,0:T(8,128)(2,1)S(1)}, bf16[68,3276]{1,0:T(8,128)(2,1)S(1)}, u32[]{:S(2)}, u32[]{:S(2)}) collective-permute-start(bf16[68,3276]{1,0:T(8,128)(2,1)S(1)} %pad_maximum_fusion.21), channel_id=1, source_target_pairs={{0,8},{4,12},{8,0},{12,4},{16,24},{20,28},{24,16},{28,20},{1,9},{5... | collective-permute-start | bytes 1336616 | tf_op jit(solution)/shard_map/ppermute | solution.py:266
  (79 other events, 1266.4 us)
Sparse Core Ops, SparseCore 0:
  11.4 94.2 all-gather.3
  109.1 88.1 all-gather.5
  200.1 82.9 all-gather.7
  421.1 143.5 reduce-scatter.3

commit v3 on v2

--- a/solution.py
+++ b/solution.py
@@ -9,6 +9,7 @@
 HEAD_DIM = 64
 FF = 4352
 LANES = 8
+KV_WIDE = 1152
 SWAP = ((0, 1), (1, 0))
 OWNERS = ("dp", "y")
 
@@ -40,8 +41,13 @@
     )
 
 
-def smooth_gate(values):
-    return jax.nn.gelu(values, approximate=True)
+def gate_and_slope(values):
+    rate = (2.0 / jnp.pi) ** 0.5
+    square = values * values
+    bend = jnp.tanh(rate * values * (1.0 + 0.044715 * square))
+    share = 0.5 * (1.0 + bend)
+    slope = share + 0.5 * values * (1.0 - bend * bend) * rate * (1.0 + 0.134145 * square)
+    return values * share, slope
 
 
 def pack_small(values, width):
@@ -83,12 +89,14 @@
     full = HEADS // 2
 
     def step(number, carry):
-        one_pair(pl.ds(pl.multiple_of(number * wide, wide), wide), 2 * number, 2)
+        start = pl.multiple_of(number * wide, wide)
+        one_pair(pl.ds(start, wide), pl.ds(KV_WIDE + start, wide), 2 * number, 2)
         return carry
 
     lax.fori_loop(0, full, step, 0)
     if HEADS % 2:
-        one_pair(pl.ds(full * wide, HEAD_DIM), 2 * full, 1)
+        start = full * wide
+        one_pair(pl.ds(start, HEAD_DIM), pl.ds(KV_WIDE + start, HEAD_DIM), 2 * full, 1)
 
 
 def only_head(values, number, heads):
@@ -113,12 +121,12 @@
     low_bias[...] = bias_of(key_ref[: 2 * half], query_ref[:, :half])
     up_bias[...] = bias_of(key_ref[2 * half :], query_ref[:, half:])
 
-    def one_pair(lanes, first, heads):
+    def one_pair(lanes, vlanes, first, heads):
         q = q_ref[:, lanes] * jnp.asarray(HEAD_DIM**-0.5, jnp.bfloat16)
-        k_low = jnp.concatenate([own_ref[0, :half, lanes], other_ref[0, :half, lanes]], axis=0)
-        k_up = jnp.concatenate([own_ref[0, half:, lanes], other_ref[0, half:, lanes]], axis=0)
-        v_low = jnp.concatenate([own_ref[1, :half, lanes], other_ref[1, :half, lanes]], axis=0).T
-        v_up = jnp.concatenate([own_ref[1, half:, lanes], other_ref[1, half:, lanes]], axis=0).T
+        k_low = jnp.concatenate([own_ref[:half, lanes], other_ref[:half, lanes]], axis=0)
+        k_up = jnp.concatenate([own_ref[half:, lanes], other_ref[half:, lanes]], axis=0)
+        v_low = jnp.concatenate([own_ref[:half, vlanes], other_ref[:half, vlanes]], axis=0).T
+        v_up = jnp.concatenate([own_ref[half:, vlanes], other_ref[half:, vlanes]], axis=0).T
         low_parts, up_parts = [], []
         for number in range(heads):
             rows = slice(number * HEAD_DIM, (number + 1) * HEAD_DIM)
@@ -168,7 +176,7 @@
     low_bias[...] = bias_of(key_ref[: 2 * half], query_ref[:, :half])
     up_bias[...] = bias_of(key_ref[2 * half :], query_ref[:, half:])
 
-    def one_pair(lanes, first, heads):
+    def one_pair(lanes, vlanes, first, heads):
         q = q_ref[:, lanes] * jnp.asarray(factor, jnp.bfloat16)
         grad = grad_ref[:, lanes]
         product = (grad.astype(jnp.float32) * mixed_ref[:, lanes].astype(jnp.float32)).T
@@ -185,8 +193,8 @@
             bias_rows = slice(place * half, (place + 1) * half)
             for upper in (False, True):
                 rows = slice(half, None) if upper else slice(0, half)
-                k = source[0, rows, lanes]
-                v = source[1, rows, lanes]
+                k = source[rows, lanes]
+                v = source[rows, vlanes]
                 k_turned = k.T
                 dk_parts, dv_parts = [], []
                 for number in range(heads):
@@ -210,8 +218,8 @@
                     if low is not None:
                         dq_low[number] = low if dq_low[number] is None else dq_low[number] + low
                     dq_up[number] = up if dq_up[number] is None else dq_up[number] + up
-                out[0, rows, lanes] = join_heads(dk_parts).astype(jnp.bfloat16)
-                out[1, rows, lanes] = join_heads(dv_parts).astype(jnp.bfloat16)
+                out[rows, lanes] = join_heads(dk_parts).astype(jnp.bfloat16)
+                out[rows, vlanes] = join_heads(dv_parts).astype(jnp.bfloat16)
         dq_ref[:half, lanes] = (jnp.concatenate(dq_low, axis=0).T * factor).astype(jnp.bfloat16)
         dq_ref[half:, lanes] = (jnp.concatenate(dq_up, axis=0).T * factor).astype(jnp.bfloat16)
 
@@ -226,6 +234,30 @@
         compiler_params=pltpu.CompilerParams(vmem_limit_bytes=48 * 1024 * 1024),
         cost_estimate=pl.CostEstimate(flops=cost, bytes_accessed=12 << 20, transcendentals=cost // 256),
     )
+
+
+def outer_kernel(left_ref, right_ref, out_ref):
+    out_ref[...] = lead_dot(left_ref[...], right_ref[...]).astype(out_ref.dtype)
+
+
+def outer(left, right):
+    rows, count = left.shape
+    width = right.shape[1]
+    step = 256
+    return pl.pallas_call(
+        outer_kernel,
+        grid=(count // step,),
+        in_specs=[
+            pl.BlockSpec((rows, step), lambda i: (0, i)),
+            pl.BlockSpec((rows, width), lambda i: (0, 0)),
+        ],
+        out_specs=pl.BlockSpec((step, width), lambda i: (i, 0)),
+        out_shape=jax.ShapeDtypeStruct((count, width), jnp.bfloat16),
+        compiler_params=pltpu.CompilerParams(vmem_limit_bytes=32 * 1024 * 1024),
+        cost_estimate=pl.CostEstimate(
+            flops=2 * rows * count * width, bytes_accessed=16 << 20, transcendentals=0
+        ),
+    )(left, right)
 
 
 def attend(query, own, other, query_places, key_places):
@@ -278,11 +310,21 @@
     return (owner ^ far) * each + inner
 
 
-def halve_first(left, right, order):
+def give_first(left, right, order):
     half = left.shape[1] // 2
-    give = round_low(lead_dot(left[:, half:], right))
-    got = swap_with(give, *order[0])
+    return swap_with(round_low(lead_dot(left[:, half:], right)), *order[0])
+
+
+def keep_first(left, right, got):
+    half = left.shape[1] // 2
     return round_low(lead_dot(left[:, :half], right) + got.astype(jnp.float32))
+
+
+def double(values, axis, bit):
+    return jnp.concatenate([values, swap_with(values, axis, bit)], axis=0)
+
+
+tie = lax.optimization_barrier
 
 
 def halve(values, axis, bit):
@@ -320,7 +362,13 @@
         return jnp.stack([first, second])
 
     inputs = trade(tokens)
-    if whole_rows:
+    grad_rows = trade(cotangent)
+    if whole_rows:
+        steps = [("dp", bit) for bit in range(dp_bits)]
+        order_a = [("core", 0), steps[0], ("y", 0)] + steps[1:]
+        order_b = [("core", 0), ("y", 0), steps[0]] + steps[1:]
+        turn_a = one_hot_columns(near_owners(order_a, dp_bits, each), model_width)
+        turn_b = one_hot_columns(near_owners(order_b, dp_bits, each), model_width)
         blocks = jnp.concatenate(
             [w_qkv.reshape(each, 3 * model_width), w_out.reshape(each, model_width)], axis=1
         )
@@ -329,10 +377,17 @@
         extra = jnp.pad(small_params.reshape(1, -1), [(0, room), (0, FF - small_len)])
         extra = extra.reshape(1 + room, FF)
         blocks = jnp.concatenate([blocks, extra], axis=0)
-        up_block = jnp.pad(w_up.reshape(each, FF), [(0, held - each), (0, 0)])
         blocks = lax.all_gather(blocks, ALL, axis=0, tiled=True)
-        up_mat = lax.all_gather(up_block, ALL, axis=0, tiled=True)
         down_mat = lax.all_gather(w_down.reshape(-1, model_width), ALL, axis=0, tiled=True)
+        up_part = w_up.reshape(each, FF)
+        for step in order_a[:2:-1]:
+            up_part = double(up_part, *step)
+        up_cut = FF // 2
+        up_a = double(up_part[:, :up_cut], *order_a[2])
+        up_b = double(up_part[:, up_cut:], *order_b[2])
+        up_a = double(up_a, *order_a[1])
+        up_b = double(up_b, *order_b[1])
+        blocks, up_a, up_b = tie((blocks, up_a, up_b))
         qkv_mat = blocks[:, : 3 * model_width]
         out_mat = blocks[:, 3 * model_width :]
         packed = blocks.reshape(owners, held, FF)[:, each, :small_len].reshape(-1)
@@ -346,6 +401,9 @@
 
         def narrow(values):
             return tail_dot(round_low(values), spread)
+
+        def turned(values):
+            return round_low(dot_rows(values, turn_a)), round_low(dot_rows(values, turn_b))
 
     else:
         small_width = -(-small_len // LANES)
@@ -366,7 +424,13 @@
         def narrow(values):
             return values
 
-    grad_rows = trade(cotangent)
+        def send_sum(left, right, extra=None):
+            grad = round_low(lead_dot(left, right)).reshape(groups * 2, 2, LANES, -1)
+            if extra is not None:
+                extra = extra.reshape(groups * 2, 2, small_len)
+                grad = jnp.concatenate([grad, pack_small(extra, small_width)], axis=-1)
+            return scatter_packed(grad, core)
+
     packed = packed.astype(jnp.float32)
     pieces = [packed[number * model_width : (number + 1) * model_width] for number in range(7)]
     gain_one, bias_one, bias_query, bias_value, bias_out, gain_two, bias_two = pieces
@@ -391,75 +455,107 @@
     qkv_bias = jnp.concatenate([bias_query, jnp.zeros_like(bias_query), bias_value])
     qkv_rows = round_low(dot_rows(widen(act_one), qkv_mat) + qkv_bias)
     query = qkv_rows[:, :model_width]
-    own_kv = jnp.stack([qkv_rows[:, model_width : 2 * model_width], qkv_rows[:, 2 * model_width :]])
+    spare = jnp.zeros((rows, KV_WIDE - model_width), jnp.bfloat16)
+    own_kv = jnp.concatenate(
+        [qkv_rows[:, model_width : 2 * model_width], spare, qkv_rows[:, 2 * model_width :], spare],
+        axis=1,
+    )
     other_kv = lax.ppermute(own_kv, "core", SWAP)
     mixed, logs = attend(query, own_kv, other_kv, query_places, key_places)
+    if whole_rows:
+        up_a = double(up_a, *order_a[0])
+        up_b = double(up_b, *order_b[0])
+        mixed, up_a, up_b = tie((mixed, up_a, up_b))
     resid = inputs + dot_rows(widen(mixed), out_mat) + bias_out
     normed_two, inverse_two = layer_stats(resid)
     act_two = round_low(normed_two * gain_two + bias_two)
-    pre_act = dot_rows(widen(act_two), up_mat) + up_bias
-    gelu_rows = round_low(smooth_gate(pre_act))
+    if whole_rows:
+        two_a, two_b = turned(act_two)
+        gelu_a, slope_a = gate_and_slope(dot_rows(two_a, up_a) + up_bias[:up_cut])
+        gelu_b, slope_b = gate_and_slope(dot_rows(two_b, up_b) + up_bias[up_cut:])
+        slopes = [round_low(slope_a), round_low(slope_b)]
+        gelu_rows = jnp.concatenate([round_low(gelu_a), round_low(gelu_b)], axis=1)
+    else:
+        gelu_rows, slope = gate_and_slope(dot_rows(act_two, up_mat) + up_bias)
+        slopes = [round_low(slope)]
+        gelu_rows = round_low(gelu_rows)
+    sum_down = outer(gelu_rows, grad_rows)
+    gelu_rows, sum_down, slopes = tie((gelu_rows, sum_down, slopes))
+    sum_down = sum_down.reshape(owners, -1, model_width)
+    sum_down = lax.psum_scatter(sum_down, ALL, scatter_dimension=0, tiled=True)
     outputs = resid + dot_rows(gelu_rows, down_mat) + down_bias
     result = trade_back(round_low(outputs))
 
-    if whole_rows:
-        steps = [("dp", bit) for bit in range(dp_bits)]
-        order_a = [("core", 0), steps[0], ("y", 0)] + steps[1:]
-        order_b = [("core", 0), ("y", 0), steps[0]] + steps[1:]
-        turn_a = one_hot_columns(near_owners(order_a, dp_bits, each), model_width)
-        turn_b = one_hot_columns(near_owners(order_b, dp_bits, each), model_width)
-
-        def send_sum(left, right, extra=None):
-            cut = (right.shape[1] // 256) * 128
-            left_a = round_low(dot_rows(left, turn_a))
-            left_b = round_low(dot_rows(left, turn_b))
-            part_a = halve_first(left_a, right[:, :cut], order_a)
-            part_b = halve_first(left_b, right[:, cut:], order_b)
-            if extra is not None:
-                extra = extra.reshape(model_width, -1)
-                extra = round_low(lead_dot(turn_b, extra))
-                part_b = jnp.concatenate([part_b, halve(extra, *order_b[0])], axis=1)
-            for step_a, step_b in zip(order_a[1:3], order_b[1:3]):
-                part_a, part_b = halve(part_a, *step_a), halve(part_b, *step_b)
-            part = jnp.concatenate([part_a, part_b], axis=1)
-            for step in order_a[3:]:
-                part = halve(part, *step)
-            return part
-
+    grad_float = grad_rows.astype(jnp.float32)
+    down_bias_term = jnp.sum(grad_float, axis=0)
+    wide = FF // len(slopes)
+    grad_pre = [
+        round_low(
+            tail_dot(grad_rows, down_mat[number * wide : (number + 1) * wide])
+            * slope.astype(jnp.float32)
+        )
+        for number, slope in enumerate(slopes)
+    ]
+    up_bias_term = jnp.concatenate(
+        [jnp.sum(part.astype(jnp.float32), axis=0) for part in grad_pre]
+    )
+    if whole_rows:
+        pre_a, pre_b = grad_pre
+        got_a = give_first(two_a, pre_a, order_a)
+        got_b = give_first(two_b, pre_b, order_b)
+        back_a, back_b = tail_dot(pre_a, up_a), tail_dot(pre_b, up_b)
+        back_a, back_b, got_a, got_b = tie((back_a, back_b, got_a, got_b))
+        sum_a = keep_first(two_a, pre_a, got_a)
+        sum_b = keep_first(two_b, pre_b, got_b)
+        back_a, back_b, sum_a, sum_b = tie((back_a, back_b, sum_a, sum_b))
+        grad_act_two = tail_dot(round_low(back_a), turn_a) + tail_dot(round_low(back_b), turn_b)
     else:
-
-        def send_sum(left, right, extra=None):
-            grad = round_low(lead_dot(left, right)).reshape(groups * 2, 2, LANES, -1)
-            if extra is not None:
-                extra = extra.reshape(groups * 2, 2, small_len)
-                grad = jnp.concatenate([grad, pack_small(extra, small_width)], axis=-1)
-            return scatter_packed(grad, core)
-
-    grad_float = grad_rows.astype(jnp.float32)
-    sum_down = round_low(lead_dot(gelu_rows, grad_rows)).reshape(owners, -1, model_width)
-    sum_down = lax.psum_scatter(sum_down, ALL, scatter_dimension=0, tiled=True)
-    down_bias_term = jnp.sum(grad_float, axis=0)
-    grad_gelu = tail_dot(grad_rows, down_mat)
-    gelu_pull = jax.vjp(smooth_gate, pre_act)[1]
-    grad_pre = round_low(gelu_pull(grad_gelu)[0])
-    sum_up = send_sum(act_two, grad_pre)
-    up_bias_term = jnp.sum(grad_pre.astype(jnp.float32), axis=0)
-    grad_act_two = narrow(tail_dot(grad_pre, up_mat))
+        sum_up = send_sum(act_two, grad_pre[0])
+        grad_act_two = tail_dot(grad_pre[0], up_mat)
     gain_two_term = jnp.sum(grad_act_two * normed_two, axis=0)
     bias_two_term = jnp.sum(grad_act_two, axis=0)
     grad_resid = grad_float + norm_back(grad_act_two, normed_two, inverse_two, gain_two)
     grad_attn = round_low(grad_resid)
-    sum_out = send_sum(mixed, grad_attn)
     bias_out_term = jnp.sum(grad_attn.astype(jnp.float32), axis=0)
+    if whole_rows:
+        out_cut = (model_width // 256) * 128
+        mixed_a, mixed_b = turned(mixed)
+        out_got_a = give_first(mixed_a, grad_attn[:, :out_cut], order_a)
+        out_got_b = give_first(mixed_b, grad_attn[:, out_cut:], order_b)
+    else:
+        sum_out = send_sum(mixed, grad_attn)
     grad_mixed = round_low(narrow(tail_dot(grad_attn, out_mat)))
+    if whole_rows:
+        out_a = keep_first(mixed_a, grad_attn[:, :out_cut], out_got_a)
+        out_b = keep_first(mixed_b, grad_attn[:, out_cut:], out_got_b)
+        grad_mixed, out_a, out_b = tie((grad_mixed, out_a, out_b))
     grad_query, grad_own, grad_other = attend_back(
         query, own_kv, other_kv, query_places, key_places, mixed, logs, grad_mixed
     )
+    if whole_rows:
+        sum_a, sum_b = halve(sum_a, *order_a[1]), halve(sum_b, *order_b[1])
+        out_a, out_b = halve(out_a, *order_a[1]), halve(out_b, *order_b[1])
+        grad_other, sum_a, sum_b, out_a, out_b = tie((grad_other, sum_a, sum_b, out_a, out_b))
+        one_a, one_b = turned(act_one)
     grad_got = lax.ppermute(grad_other, "core", SWAP)
     grad_kv = round_low(grad_own.astype(jnp.float32) + grad_got.astype(jnp.float32))
-    grad_qkv_rows = jnp.concatenate([grad_query, grad_kv[0], grad_kv[1]], axis=1)
+    grad_qkv_rows = jnp.concatenate(
+        [grad_query, grad_kv[:, :model_width], grad_kv[:, KV_WIDE : KV_WIDE + model_width]], axis=1
+    )
     qkv_sums = jnp.sum(grad_qkv_rows.astype(jnp.float32), axis=0)
+    if whole_rows:
+        qkv_cut = (3 * model_width // 256) * 128
+        rows_a, rows_b = grad_qkv_rows[:, :qkv_cut], grad_qkv_rows[:, qkv_cut:]
+        qkv_got_a = give_first(one_a, rows_a, order_a)
+        qkv_got_b = give_first(one_b, rows_b, order_b)
     grad_act_one = narrow(tail_dot(grad_qkv_rows, qkv_mat))
+    if whole_rows:
+        sum_a, sum_b = halve(sum_a, *order_a[2]), halve(sum_b, *order_b[2])
+        out_a, out_b = halve(out_a, *order_a[2]), halve(out_b, *order_b[2])
+        rest = jnp.concatenate([sum_a, sum_b, out_a, out_b], axis=1)
+        qkv_a = keep_first(one_a, rows_a, qkv_got_a)
+        qkv_b = keep_first(one_b, rows_b, qkv_got_b)
+        rest, qkv_a, qkv_b, grad_act_one = tie((rest, qkv_a, qkv_b, grad_act_one))
     gain_one_term = jnp.sum(grad_act_one * normed_one, axis=0)
     bias_one_term = jnp.sum(grad_act_one, axis=0)
     small_grad = jnp.concatenate(
@@ -475,9 +571,29 @@
             down_bias_term,
         ]
     )
-    sum_qkv = send_sum(act_one, grad_qkv_rows, round_low(small_grad))
+    small_grad = round_low(small_grad)
     grad_input = grad_resid + norm_back(grad_act_one, normed_one, inverse_one, gain_one)
-    grad_tokens = trade_back(round_low(grad_input))
+    grad_input = round_low(grad_input)
+    if whole_rows:
+        small_rows = round_low(lead_dot(turn_a, small_grad.reshape(model_width, -1)))
+        small_rows = halve(small_rows, *order_a[0])
+        qkv_a, qkv_b = halve(qkv_a, *order_a[1]), halve(qkv_b, *order_b[1])
+        rest = halve(rest, *order_a[3])
+        grad_input, qkv_a, qkv_b, rest, small_rows = tie(
+            (grad_input, qkv_a, qkv_b, rest, small_rows)
+        )
+        qkv_a, qkv_b = halve(qkv_a, *order_a[2]), halve(qkv_b, *order_b[2])
+        small_rows = halve(halve(small_rows, *order_a[1]), *order_a[2])
+        for step in order_a[4:]:
+            rest = halve(rest, *step)
+        qkv_a, qkv_b, rest, small_rows = tie((qkv_a, qkv_b, rest, small_rows))
+        sum_qkv = jnp.concatenate([qkv_a, qkv_b, small_rows], axis=1)
+        for step in order_a[3:]:
+            sum_qkv = halve(sum_qkv, *step)
+        sum_up, sum_out = rest[:, :FF], rest[:, FF:]
+    else:
+        sum_qkv = send_sum(act_one, grad_qkv_rows, small_grad)
+    grad_tokens = trade_back(grad_input)
     main = w_qkv.shape[0] // sum_qkv.shape[0]
     grad_qkv = sum_qkv[:, :main].astype(jnp.float32).reshape(-1)
     grad_small = sum_qkv[:, main:].astype(jnp.float32).reshape(-1)[:small_len]

time: 642 us -> 589 us (0.917)
  waiting for transfers between devices: 268 us -> 148 us
  other arithmetic: 35.2 us -> 70.9 us
  starting transfers between devices: 28.5 us -> 48.4 us
  Pallas kernels: 43.8 us -> 55.4 us
  matrix products: 156 us -> 145 us
  local copies, waits for them, and re-layouts: 85 us -> 94.2 us
    all_gather x1, waiting for transfers between devices: 69.6 us -> 0.01 us  [local(): lax.all_gather(w_down.reshape(-1, model_width), ALL, axis=0, tiled=True)]
    all_gather x1, waiting for transfers between devices: 70.6 us -> 2.61 us  [local(): blocks = lax.all_gather(blocks, ALL, axis=0, tiled=True)]
    ppermute x25 -> x33, waiting for transfers between devices: 107 us -> 146 us  [swap_with(): lax.ppermute(values, axis, [(here, here ^ 1 << bit) for here in range(cou...]
    ppermute x25 -> x33, starting transfers between devices: 22.8 us -> 43.7 us  [swap_with(): lax.ppermute(values, axis, [(here, here ^ 1 << bit) for here in range(cou...]
    concatenate x4 -> x11, other arithmetic: 0.42 us -> 16.7 us  [the longest x8 12.8 us: double(): return jnp.concatenate([values, swap_with(values, axis, bit)], axis=0)]
    convert_element_type x3 -> x1, local copies, waits for them, and re-layouts: 16.7 us -> 2.08 us  [round_low(): return values.astype(jnp.bfloat16)]
    unnamed x143 -> x251, local copies, waits for them, and re-layouts: 16 us -> 29.2 us
    convert_element_type x20 -> x24, other arithmetic: 11.1 us -> 23.7 us  [round_low(): return values.astype(jnp.bfloat16)]
  transfers between devices with their start and end apart: 35 -> 42, of which waited for: 18 -> 14; matrix products, arithmetic and copies ran while one was open for 39% -> 46% of each run, Pallas kernels for 7% -> 10%
where the time goes in v3:
time: 589 us; the launch traced here: 578 us
  waiting for transfers between devices  148 us (25%)
  matrix products  145 us (25%)
  local copies, waits for them, and re-layouts  94.2 us (16%)
  other arithmetic  70.9 us (12%)
  Pallas kernels  55.4 us (9%)
  starting transfers between devices  48.4 us (8%)
  between operations  15.7 us (3%)
    ppermute x33, waiting for transfers between devices, swap_with(): lax.ppermute(values, axis, [(here, here ^ 1 << bit) for here in range(cou...  146 us
    dot_general x11, matrix products, dot_rows(): lax.dot_general(left, right, (((1,), (0,)), ((), ())), preferred_element_...  56.4 us
    dot_general x8, matrix products, tail_dot(): lax.dot_general(left_side, right_side, (((1,), (1,)), ((), ())), preferre...  52.4 us
    ppermute x33, starting transfers between devices, swap_with(): lax.ppermute(values, axis, [(here, here ^ 1 << bit) for here in range(cou...  43.7 us
    dot_general x13, matrix products, lead_dot(): lax.dot_general(left_side, right_side, (((0,), (0,)), ((), ())), preferre...  36.5 us
    unnamed x251, local copies, waits for them, and re-layouts  29.2 us
    pallas_call x1, Pallas kernels, attend_back(): return call(query, own, other, query_places, key_places, mixed, logs, grad)  26.9 us
    convert_element_type x24, other arithmetic, round_low(): return values.astype(jnp.bfloat16)  23.7 us
  transfers between devices with their start and end apart: 42, of which 14 were waited for; matrix products, arithmetic and copies ran while one was open for 46% of the time, Pallas kernels for 10%

profile of v3, /device:TPU:0, one launch (start us, length us, event | category | flops | bytes accessed | tf_op | source)
XLA Modules:
  0.0 578.0 jit_solution(7893963603386454740)
XLA Ops:
  22.7 17.0 %collective-permute-done.1 = bf16[34,4352]{1,0:T(8,128)(2,1)S(1)} collective-permute-done((bf16[34,4352]{1,0:T(8,128)(2,1)S(1)}, bf16[34,4352]{1,0:T(8,128)(2,1)S(1)}, u32[]{:S(2)}, u32[]{:S(2)}) %collective-permute-start.1) | collective-permute-done | bytes 295968 | tf_op jit(solution)/shard_map/ppermute | solution.py:298
  49.2 19.2 %collective-permute-done.2 = bf16[68,4352]{1,0:T(8,128)(2,1)} collective-permute-done((bf16[68,4352]{1,0:T(8,128)(2,1)}, bf16[68,4352]{1,0:T(8,128)(2,1)}, u32[]{:S(2)}, u32[]{:S(2)}) %collective-permute-start.2) | collective-permute-done | bytes 591904 | tf_op jit(solution)/shard_map/ppermute | solution.py:298
  78.4 9.6 %collective-permute-done.3 = bf16[136,2176]{1,0:T(8,128)(2,1)S(1)} collective-permute-done((bf16[136,2176]{1,0:T(8,128)(2,1)S(1)}, bf16[136,2176]{1,0:T(8,128)(2,1)S(1)}, u32[]{:S(2)}, u32[]{:S(2)}) %collective-permute-start.3) | collective-permute-done | bytes 591904 | tf_op jit(solution)/shard_map/ppermute | solution.py:298
  88.8 11.5 %collective-permute-done.5 = bf16[136,2176]{1,0:T(8,128)(2,1)S(1)} collective-permute-done((bf16[136,2176]{1,0:T(8,128)(2,1)S(1)}, bf16[136,2176]{1,0:T(8,128)(2,1)S(1)}, u32[]{:S(2)}, u32[]{:S(2)}) %collective-permute-start.5) | collective-permute-done | bytes 591904 | tf_op jit(solution)/shard_map/ppermute | solution.py:298
  101.9 27.8 %collective-permute-done.4 = bf16[272,2176]{1,0:T(8,128)(2,1)S(1)} collective-permute-done((bf16[272,2176]{1,0:T(8,128)(2,1)S(1)}, bf16[272,2176]{1,0:T(8,128)(2,1)S(1)}, u32[]{:S(2)}, u32[]{:S(2)}) %collective-permute-start.4) | collective-permute-done | bytes 1183776 | tf_op jit(solution)/shard_map/ppermute | solution.py:298
  137.7 11.8 %add_convert_fusion = bf16[512,3264]{1,0:T(8,128)(2,1)} fusion(bf16[1280,4352]{1,0:T(8,128)(2,1)} %all-gather.3.cloned.1.call-done, f32[3264]{0:T(1024)S(1)} %concatenate.98, s32[1280]{0:T(1024)S(1)} %copy-done.86, f32[1088]{0:T(1024)S(1)} %get-tuple-element.177, f32[1088]{0:T(1024)S(1)} %get-tuple-element.178, f32[512]{0:T(512)S(1)} %copy-done.73, ...), kind=kOutput, calls=%fused_computation.4 | convolution fusion | flops 5716885504 | bytes 13007104 | tf_op jit(solution)/shard_map/dot_general | solution.py:78
  186.6 18.8 %shard_map.135 = (bf16[512,1088]{1,0:T(8,128)(2,1)S(1)}, f32[17,512]{1,0:T(8,128)S(1)}) custom-call(bf16[512,1088]{1,0:T(8,128)(2,1)S(1)} %get-tuple-element.146.q_ref, bf16[512,2304]{1,0:T(8,128)(2,1)S(1)} %concatenate.99.own_ref, bf16[512,2304]{1,0:T(8,128)(2,1)} %collective-permute-done.7.other_ref, s32[1,512]{1,0:T(1,128)S(1)} %bitcast.75, ...), custom_call_target="tpu_custom_call" | custom-call | flops 8589934592 | bytes 12582912 | tf_op jit(solution)/shard_map/pallas_call | solution.py:270
  212.6 7.6 %fusion.149 = (f32[512]{0:T(512)}, f32[512,1088]{1,0:T(8,128)}) fusion(f32[1088]{0:T(1024)S(1)} %copy-done.83, bf16[1280,4352]{1,0:T(8,128)(2,1)} %all-gather.3.cloned.1.call-done, bf16[512,1088]{1,0:T(8,128)(2,1)S(1)} %copy-done.7, s32[1280]{0:T(1024)} %fusion.123, bf16[128,1088]{1,0:T(8,128)(2,1)S(1)} %copy-done.29, bf16[128,1088]{1,0:T(8,128)(2,1)S(1)} %bitcast.84, ...), kind=kOutput, calls=%fused_computation.268 | convolution fusion | flops 2860301824 | bytes 7420160 | tf_op jit(solution)/shard_map/dot_general | solution.py:78
  227.6 7.4 %add_convert_fusion.4 = (bf16[512,2176]{1,0:T(8,128)(2,1)}, bf16[512,2176]{1,0:T(8,128)(2,1)S(1)}) fusion(f32[2176]{0:T(1024)S(1)} %copy-done.79, bf16[512,1088]{0,1:T(8,128)(2,1)S(1)} %fusion.34, bf16[1088,2176]{1,0:T(8,128)(2,1)S(1)} %bitcast.96), kind=kOutput, calls=%fused_computation.37 | convolution fusion | flops 2446589952 | bytes 10314240 | tf_op jit(solution)/shard_map/dot_general | solution.py:78
  235.1 6.9 %add_convert_fusion.5 = (bf16[512,2176]{1,0:T(8,128)(2,1)}, bf16[512,2176]{1,0:T(8,128)(2,1)S(1)}) fusion(f32[2176]{0:T(1024)S(1)} %copy-done.78, bf16[512,1088]{0,1:T(8,128)(2,1)S(1)} %fusion.31, bf16[1088,2176]{1,0:T(8,128)(2,1)S(1)} %bitcast.98), kind=kOutput, calls=%fused_computation.38 | convolution fusion | flops 2446589952 | bytes 10314240 | tf_op jit(solution)/shard_map/dot_general | solution.py:78
  243.3 9.6 %shard_map.136 = bf16[4352,1088]{1,0:T(8,128)(2,1)S(1)} custom-call(bf16[512,4352]{1,0:T(8,128)(2,1)S(1)} %pad_maximum_fusion.2.left_ref, bf16[512,1088]{1,0:T(8,128)(2,1)S(1)} %copy-done.3), custom_call_target="tpu_custom_call" | custom-call | flops 4848615424 | bytes 16777216 | tf_op jit(solution)/shard_map/pallas_call | solution.py:247
  256.7 7.0 %fusion.150 = (bf16[2176]{0:T(1024)(128)(2,1)}, bf16[512,2176]{1,0:T(8,128)(2,1)S(1)}) fusion(bf16[512,2176]{1,0:T(8,128)(2,1)} %get-tuple-element.59, bf16[4352,1088]{1,0:T(8,128)(2,1)} %all-gather.5.cloned.1.call-done, bf16[128,1088]{1,0:T(8,128)(2,1)S(1)} %copy-done.41, bf16[128,1088]{1,0:T(8,128)(2,1)S(1)} %bitcast.100, ...), kind=kOutput, calls=%fused_computation.269 | convolution fusion | flops 2433218560 | bytes 10588416 | tf_op jit(solution)/shard_map/dot_general | solution.py:39
  263.7 6.3 %fusion.152 = bf16[512,1088]{0,1:T(8,128)(2,1)} fusion(bf16[512,2176]{1,0:T(8,128)(2,1)S(1)} %get-tuple-element.187, bf16[1088,2176]{1,0:T(8,128)(2,1)} %pad_maximum_fusion), kind=kOutput, calls=%fused_computation.271 | convolution fusion | flops 2424307712 | bytes 8077312 | tf_op jit(solution)/shard_map/dot_general | solution.py:39
  287.9 7.2 %fusion.151 = (bf16[2176]{0:T(1024)(128)(2,1)}, bf16[512,2176]{1,0:T(8,128)(2,1)S(1)}) fusion(bf16[512,2176]{1,0:T(8,128)(2,1)} %get-tuple-element.60, bf16[4352,1088]{1,0:T(8,128)(2,1)} %all-gather.5.cloned.1.call-done, bf16[128,1088]{1,0:T(8,128)(2,1)S(1)} %copy-done.41, bf16[128,1088]{1,0:T(8,128)(2,1)S(1)} %bitcast.101, ...), kind=kOutput, calls=%fused_computation.270 | convolution fusion | flops 2433218560 | bytes 10588416 | tf_op jit(solution)/shard_map/dot_general | solution.py:39
  301.4 6.1 %fusion.153 = bf16[512,1088]{0,1:T(8,128)(2,1)} fusion(bf16[512,2176]{1,0:T(8,128)(2,1)S(1)} %get-tuple-element.189, bf16[1088,2176]{1,0:T(8,128)(2,1)} %pad_maximum_fusion.1), kind=kOutput, calls=%fused_computation.272 | convolution fusion | flops 2424307712 | bytes 8077312 | tf_op jit(solution)/shard_map/dot_general | solution.py:39
  342.7 7.2 %fusion.39.grad_ref = bf16[512,1088]{1,0:T(8,128)(2,1)} fusion(s32[1280]{0:T(1024)S(1)} %copy-done.87, bf16[512,1088]{1,0:T(8,128)(2,1)} %copy-done.52, bf16[1280,4352]{1,0:T(8,128)(2,1)} %all-gather.3.cloned.1.call-done), kind=kOutput, calls=%fused_computation.66 | convolution fusion | flops 2854731776 | bytes 5248000 | tf_op jit(solution)/shard_map/dot_general | solution.py:39
  359.4 26.9 %shard_map.137 = (bf16[512,1088]{1,0:T(8,128)(2,1)S(1)}, bf16[512,2304]{1,0:T(8,128)(2,1)}, bf16[512,2304]{1,0:T(8,128)(2,1)}) custom-call(bf16[512,1088]{1,0:T(8,128)(2,1)S(1)} %get-tuple-element.146.q_ref, bf16[512,2304]{1,0:T(8,128)(2,1)} %copy-done.2, bf16[512,2304]{1,0:T(8,128)(2,1)} %collective-permute-done.7.other_ref, s32[1,512]{1,0:T(1,128)S(1)} %bitcast.76, ...), custom_call_target="tpu_custom_call" | custom-call | flops 25769803776 | bytes 12582912 | tf_op jit(solution)/shard_map/pallas_call | solution.py:281
  386.4 9.4 %collective-permute-done.18 = bf16[272,512]{1,0:T(8,128)(2,1)} collective-permute-done((bf16[272,512]{1,0:T(8,128)(2,1)}, bf16[272,512]{1,0:T(8,128)(2,1)}, u32[]{:S(2)}, u32[]{:S(2)}) %collective-permute-start.18) | collective-permute-done | bytes 278560 | tf_op jit(solution)/shard_map/ppermute | solution.py:298
  411.1 9.0 %collective-permute-done.23 = bf16[136,576]{1,0:T(8,128)(2,1)S(1)} collective-permute-done((bf16[136,576]{1,0:T(8,128)(2,1)S(1)}, bf16[136,576]{1,0:T(8,128)(2,1)S(1)}, u32[]{:S(2)}, u32[]{:S(2)}) %collective-permute-start.23) | collective-permute-done | bytes 156704 | tf_op jit(solution)/shard_map/ppermute | solution.py:298
  440.3 12.9 %fusion.6 = f32[512,1088]{0,1:T(8,128)} fusion(s32[1280]{0:T(1024)} %fusion.123, bf16[512,3264]{1,0:T(8,128)(2,1)} %concatenate.111, bf16[1280,4352]{1,0:T(8,128)(2,1)} %all-gather.3.cloned.1.call-done), kind=kOutput, calls=%fused_computation.6 | convolution fusion | flops 5706301440 | bytes 14163968 | tf_op jit(solution)/shard_map/dot_general | solution.py:39
  476.2 7.5 %concatenate.112 = bf16[13056]{0:T(1024)(128)(2,1)} concatenate(bf16[1088]{0:T(1024)(128)(2,1)} %get-tuple-element.118, bf16[1088]{0:T(1024)(128)(2,1)} %reduce_sum.162, bf16[1088]{0:T(1024)(128)(2,1)} %get-tuple-element.182, bf16[1088]{0:T(1024)(128)(2,1)} %get-tuple-element.181, bf16[1088]{0:T(1024)(128)(2,1)} %get-tuple-element.129, bf16[1088]{0:T(1024)(128)(2,1)} %get-tuple-element.116, ...), dimensions={0} | concatenate | bytes 52224 | tf_op jit(solution)/shard_map/concatenate | solution.py:561
  502.2 16.3 %collective-permute-start.34 = (bf16[34,5440]{1,0:T(8,128)(2,1)}, bf16[34,5440]{1,0:T(8,128)(2,1)}, u32[]{:S(2)}, u32[]{:S(2)}) collective-permute-start(bf16[34,5440]{1,0:T(8,128)(2,1)} %slice.468), channel_id=1, source_target_pairs={{0,16},{4,20},{8,24},{12,28},{16,0},{20,4},{24,8},{28,12},{1,17},{... | collective-permute-start | bytes 1109768 | tf_op jit(solution)/shard_map/ppermute | solution.py:298
  523.8 13.3 %collective-permute-done.34 = bf16[34,5440]{1,0:T(8,128)(2,1)} collective-permute-done((bf16[34,5440]{1,0:T(8,128)(2,1)}, bf16[34,5440]{1,0:T(8,128)(2,1)}, u32[]{:S(2)}, u32[]{:S(2)}) %collective-permute-start.34) | collective-permute-done | bytes 369952 | tf_op jit(solution)/shard_map/ppermute | solution.py:298
  557.1 10.0 %collective-permute-done.38 = bf16[34,3276]{1,0:T(8,128)(2,1)S(1)} collective-permute-done((bf16[34,3276]{1,0:T(8,128)(2,1)S(1)}, bf16[34,3276]{1,0:T(8,128)(2,1)S(1)}, u32[]{:S(2)}, u32[]{:S(2)}) %collective-permute-start.38) | collective-permute-done | bytes 222800 | tf_op jit(solution)/shard_map/ppermute | solution.py:298
  (480 shorter events, 276.0 us)
Async XLA Ops:
  7.2 128.4 %all-gather.3.cloned.1.call-start = ((), (), s32[]{:S(2)}) async-start(), calls=%async_computation.1 | async-start | bytes 11489280 | tf_op jit(solution)/shard_map/all_gather | solution.py:380
  11.1 245.6 %all-gather.5.cloned.1.call-start = ((), (), s32[]{:S(2)}) async-start(), calls=%async_computation.2 | async-start | bytes 10340352 | tf_op jit(solution)/shard_map/all_gather | solution.py:381
  12.5 27.2 %collective-permute-start.1 = (bf16[34,4352]{1,0:T(8,128)(2,1)S(1)}, bf16[34,4352]{1,0:T(8,128)(2,1)S(1)}, u32[]{:S(2)}, u32[]{:S(2)}) collective-permute-start(bf16[34,4352]{1,0:T(8,128)(2,1)S(1)} %reshape.209), channel_id=1, source_target_pairs={{0,16},{4,20},{8,24},{12,28},{16,0},{20,4},{24,8},{28,12},{1,17},{... | collective-permute-start | bytes 887816 | tf_op jit(solution)/shard_map/ppermute | solution.py:298
  17.5 57.6 %collective-permute-start = (bf16[256,1088]{0,1:T(8,128)(2,1)}, bf16[256,1088]{0,1:T(8,128)(2,1)}, u32[]{:S(2)}, u32[]{:S(2)}) collective-permute-start(bf16[256,1088]{0,1:T(8,128)(2,1)} %dynamic-slice_bitcast_fusion.1), channel_id=1, source_target_pairs={{0,2},{2,0},{1,3},{3,1},{4,6},{6,4},{5,7},{7,5},{8,10},{10,8},{9,1... | collective-permute-start | bytes 1671176 | tf_op jit(solution)/shard_map/ppermute | solution.py:353
  19.8 147.4 %collective-permute-start.10 = (bf16[256,1088]{0,1:T(8,128)(2,1)}, bf16[256,1088]{0,1:T(8,128)(2,1)}, u32[]{:S(2)}, u32[]{:S(2)}) collective-permute-start(bf16[256,1088]{0,1:T(8,128)(2,1)} %dynamic-slice_bitcast_fusion), channel_id=1, source_target_pairs={{0,2},{2,0},{1,3},{3,1},{4,6},{6,4},{5,7},{7,5},{8,10},{10,8},{9,1... | collective-permute-start | bytes 1671176 | tf_op jit(solution)/shard_map/ppermute | solution.py:353
  21.3 547.6 %reduce-scatter.4.cloned.1.call-start = ((), (), s32[]{:S(2)}) async-start(), calls=%async_computation.3 | async-start | bytes 10340352
  40.6 27.8 %collective-permute-start.2 = (bf16[68,4352]{1,0:T(8,128)(2,1)}, bf16[68,4352]{1,0:T(8,128)(2,1)}, u32[]{:S(2)}, u32[]{:S(2)}) collective-permute-start(bf16[68,4352]{1,0:T(8,128)(2,1)} %pad_maximum_fusion.19), channel_id=1, source_target_pairs={{0,8},{4,12},{8,0},{12,4},{16,24},{20,28},{24,16},{28,20},{1,9},{5... | collective-permute-start | bytes 1775624 | tf_op jit(solution)/shard_map/ppermute | solution.py:298
  73.8 26.5 %collective-permute-start.5 = (bf16[136,2176]{1,0:T(8,128)(2,1)S(1)}, bf16[136,2176]{1,0:T(8,128)(2,1)S(1)}, u32[]{:S(2)}, u32[]{:S(2)}) collective-permute-start(bf16[136,2176]{1,0:T(8,128)(2,1)S(1)} %get-tuple-element.149), channel_id=1, source_target_pairs={{0,4},{4,0},{8,12},{12,8},{16,20},{20,16},{24,28},{28,24},{1,5},{5... | collective-permute-start | bytes 1775624 | tf_op jit(solution)/shard_map/ppermute | solution.py:298
  88.1 41.7 %collective-permute-start.4 = (bf16[272,2176]{1,0:T(8,128)(2,1)S(1)}, bf16[272,2176]{1,0:T(8,128)(2,1)S(1)}, u32[]{:S(2)}, u32[]{:S(2)}) collective-permute-start(bf16[272,2176]{1,0:T(8,128)(2,1)S(1)} %pad_maximum_fusion.9), channel_id=1, source_target_pairs={{0,4},{4,0},{8,12},{12,8},{16,20},{20,16},{24,28},{28,24},{1,5},{5... | collective-permute-start | bytes 3551240 | tf_op jit(solution)/shard_map/ppermute | solution.py:298
  100.4 30.9 %collective-permute-start.6 = (bf16[272,2176]{1,0:T(8,128)(2,1)S(1)}, bf16[272,2176]{1,0:T(8,128)(2,1)S(1)}, u32[]{:S(2)}, u32[]{:S(2)}) collective-permute-start(bf16[272,2176]{1,0:T(8,128)(2,1)S(1)} %pad_maximum_fusion.10), channel_id=1, source_target_pairs={{0,2},{2,0},{1,3},{3,1},{4,6},{6,4},{5,7},{7,5},{8,10},{10,8},{9,1... | collective-permute-start | bytes 3551240 | tf_op jit(solution)/shard_map/ppermute | solution.py:298
  158.4 28.1 %collective-permute-start.7 = (bf16[512,2304]{1,0:T(8,128)(2,1)S(1)}, bf16[512,2304]{1,0:T(8,128)(2,1)}, u32[]{:S(2)}, u32[]{:S(2)}) collective-permute-start(bf16[512,2304]{1,0:T(8,128)(2,1)S(1)} %concatenate.99.own_ref), channel_id=1, source_target_pairs={{0,1},{1,0},{2,3},{3,2},{4,5},{5,4},{6,7},{7,6},{8,9},{9,8},{10,11... | collective-permute-start | bytes 7077896 | tf_op jit(solution)/shard_map/ppermute | solution.py:463
  167.0 38.4 %collective-permute-start.8 = (bf16[544,2176]{1,0:T(8,128)(2,1)}, bf16[544,2176]{1,0:T(8,128)(2,1)}, u32[]{:S(2)}, u32[]{:S(2)}) collective-permute-start(bf16[544,2176]{1,0:T(8,128)(2,1)} %pad_maximum_fusion.3), channel_id=1, source_target_pairs={{0,1},{1,0},{2,3},{3,2},{4,5},{5,4},{6,7},{7,6},{8,9},{9,8},{10,11... | collective-permute-start | bytes 7102472 | tf_op jit(solution)/shard_map/ppermute | solution.py:298
  177.3 32.7 %collective-permute-start.9 = (bf16[544,2176]{1,0:T(8,128)(2,1)S(1)}, bf16[544,2176]{1,0:T(8,128)(2,1)S(1)}, u32[]{:S(2)}, u32[]{:S(2)}) collective-permute-start(bf16[544,2176]{1,0:T(8,128)(2,1)S(1)} %copy-done.15), channel_id=1, source_target_pairs={{0,1},{1,0},{2,3},{3,2},{4,5},{5,4},{6,7},{7,6},{8,9},{9,8},{10,11... | collective-permute-start | bytes 7102472 | tf_op jit(solution)/shard_map/ppermute | solution.py:298
  286.5 29.3 %collective-permute-start.11 = (bf16[256,1088]{0,1:T(8,128)(2,1)}, bf16[256,1088]{0,1:T(8,128)(2,1)}, u32[]{:S(2)}, u32[]{:S(2)}) collective-permute-start(bf16[256,1088]{0,1:T(8,128)(2,1)} %copy.57), channel_id=1, source_target_pairs={{0,2},{2,0},{1,3},{3,1},{4,6},{6,4},{5,7},{7,5},{8,10},{10,8},{9,1... | collective-permute-start | bytes 1671176 | tf_op jit(solution)/shard_map/ppermute | solution.py:359
  287.9 32.9 %collective-permute-start.12 = (bf16[544,2176]{1,0:T(8,128)(2,1)}, bf16[544,2176]{1,0:T(8,128)(2,1)}, u32[]{:S(2)}, u32[]{:S(2)}) collective-permute-start(bf16[544,2176]{1,0:T(8,128)(2,1)} %convolution_convert_fusion.1), channel_id=1, source_target_pairs={{0,1},{1,0},{2,3},{3,2},{4,5},{5,4},{6,7},{7,6},{8,9},{9,8},{10,11... | collective-permute-start | bytes 7102472 | tf_op jit(solution)/shard_map/ppermute | solution.py:298
  351.4 49.2 %collective-permute-start.16 = (bf16[272,2176]{1,0:T(8,128)(2,1)S(1)}, bf16[272,2176]{1,0:T(8,128)(2,1)S(1)}, u32[]{:S(2)}, u32[]{:S(2)}) collective-permute-start(bf16[272,2176]{1,0:T(8,128)(2,1)S(1)} %slice.426), channel_id=1, source_target_pairs={{0,4},{4,0},{8,12},{12,8},{16,20},{20,16},{24,28},{28,24},{1,5},{5... | collective-permute-start | bytes 3551240 | tf_op jit(solution)/shard_map/ppermute | solution.py:298
  352.1 48.9 %collective-permute-start.17 = (bf16[272,2176]{1,0:T(8,128)(2,1)S(1)}, bf16[272,2176]{1,0:T(8,128)(2,1)S(1)}, u32[]{:S(2)}, u32[]{:S(2)}) collective-permute-start(bf16[272,2176]{1,0:T(8,128)(2,1)S(1)} %slice.428), channel_id=1, source_target_pairs={{0,2},{2,0},{1,3},{3,1},{4,6},{6,4},{5,7},{7,5},{8,10},{10,8},{9,1... | collective-permute-start | bytes 3551240 | tf_op jit(solution)/shard_map/ppermute | solution.py:298
  355.6 40.1 %collective-permute-start.18 = (bf16[272,512]{1,0:T(8,128)(2,1)}, bf16[272,512]{1,0:T(8,128)(2,1)}, u32[]{:S(2)}, u32[]{:S(2)}) collective-permute-start(bf16[272,512]{1,0:T(8,128)(2,1)} %slice.430), channel_id=1, source_target_pairs={{0,4},{4,0},{8,12},{12,8},{16,20},{20,16},{24,28},{28,24},{1,5},{5... | collective-permute-start | bytes 835592 | tf_op jit(solution)/shard_map/ppermute | solution.py:298
  357.8 42.0 %collective-permute-start.19 = (bf16[272,576]{1,0:T(8,128)(2,1)}, bf16[272,576]{1,0:T(8,128)(2,1)S(1)}, u32[]{:S(2)}, u32[]{:S(2)}) collective-permute-start(bf16[272,576]{1,0:T(8,128)(2,1)} %slice.432), channel_id=1, source_target_pairs={{0,2},{2,0},{1,3},{3,1},{4,6},{6,4},{5,7},{7,5},{8,10},{10,8},{9,1... | collective-permute-start | bytes 940040 | tf_op jit(solution)/shard_map/ppermute | solution.py:298
  428.6 24.6 %collective-permute-start.25 = (bf16[544,1536]{1,0:T(8,128)(2,1)}, bf16[544,1536]{1,0:T(8,128)(2,1)}, u32[]{:S(2)}, u32[]{:S(2)}) collective-permute-start(bf16[544,1536]{1,0:T(8,128)(2,1)} %convolution_convert_fusion.3), channel_id=1, source_target_pairs={{0,1},{1,0},{2,3},{3,2},{4,5},{5,4},{6,7},{7,6},{8,9},{9,8},{10,11... | collective-permute-start | bytes 5013512 | tf_op jit(solution)/shard_map/ppermute | solution.py:298
  471.4 25.4 %collective-permute-start.27 = (bf16[272,1536]{1,0:T(8,128)(2,1)}, bf16[272,1536]{1,0:T(8,128)(2,1)}, u32[]{:S(2)}, u32[]{:S(2)}) collective-permute-start(bf16[272,1536]{1,0:T(8,128)(2,1)} %slice.450), channel_id=1, source_target_pairs={{0,4},{4,0},{8,12},{12,8},{16,20},{20,16},{24,28},{28,24},{1,5},{5... | collective-permute-start | bytes 2506760 | tf_op jit(solution)/shard_map/ppermute | solution.py:298
  473.9 24.4 %collective-permute-start.28 = (bf16[272,1728]{1,0:T(8,128)(2,1)}, bf16[272,1728]{1,0:T(8,128)(2,1)}, u32[]{:S(2)}, u32[]{:S(2)}) collective-permute-start(bf16[272,1728]{1,0:T(8,128)(2,1)} %slice.452), channel_id=1, source_target_pairs={{0,2},{2,0},{1,3},{3,1},{4,6},{6,4},{5,7},{7,5},{8,10},{10,8},{9,1... | collective-permute-start | bytes 2820104 | tf_op jit(solution)/shard_map/ppermute | solution.py:298
  502.2 34.9 %collective-permute-start.34 = (bf16[34,5440]{1,0:T(8,128)(2,1)}, bf16[34,5440]{1,0:T(8,128)(2,1)}, u32[]{:S(2)}, u32[]{:S(2)}) collective-permute-start(bf16[34,5440]{1,0:T(8,128)(2,1)} %slice.468), channel_id=1, source_target_pairs={{0,16},{4,20},{8,24},{12,28},{16,0},{20,4},{24,8},{28,12},{1,17},{... | collective-permute-start | bytes 1109768 | tf_op jit(solution)/shard_map/ppermute | solution.py:298
  520.8 27.1 %collective-permute-start.31 = (bf16[256,1088]{0,1:T(8,128)(2,1)}, bf16[256,1088]{0,1:T(8,128)(2,1)}, u32[]{:S(2)}, u32[]{:S(2)}) collective-permute-start(bf16[256,1088]{0,1:T(8,128)(2,1)} %copy.67), channel_id=1, source_target_pairs={{0,2},{2,0},{1,3},{3,1},{4,6},{6,4},{5,7},{7,5},{8,10},{10,8},{9,1... | collective-permute-start | bytes 1671176 | tf_op jit(solution)/shard_map/ppermute | solution.py:359
  (135 other events, 1303.3 us)
Sparse Core Ops, SparseCore 0:
  11.4 124.0 all-gather.2
  139.0 82.8 all-gather.4
  310.5 155.3 reduce-scatter.3
